TPU v7x, 512 devices: a whole 4x4x16 slice. The times are simulated.
512 devices in a mesh: seq: 32 (over z, core), mp: 16 (over y, x).
Axes of the slice: x: 4, y: 4, z: 16, core: 2. Of those that a mesh axis runs over, the one named last changes fastest.
Arguments:
- residual: bfloat16 [4096, 8192], P('seq', 'mp'), may hold values from -6 to 6
- hyena_streams: bfloat16 [4096, 3, 8192], P('seq', None, 'mp'), may hold values from -6 to 6
- hyena_filter: float32 [7, 8192], P(None, 'mp'), may hold values from -3 to 3
- attention_streams: bfloat16 [4096, 3, 8192], P('seq', None, 'mp'), may hold values from -4.5 to 4.5
- norm_gain: float32 [8192], P('mp'), may hold values from 0.5 to 1.5
- record_starts: int32 [16], replicated, may hold values from 0 to 4095, as said below
- record_lengths: int32 [16], replicated, may hold values from 1 to 2048, as said below
- segment_ids: int32 [4096], P('seq'), may hold values from 0 to 15, as said below
Outputs:
- mixed: float32 [4096, 8192], P('seq', 'mp')
- record_energy: float32 [16], replicated
Inputs may be any that keep to these rules, and one draw needn't show every extreme that they name: Records lie end to end from position 0: record_starts[r] is the sum of record_lengths of the records before r, and they cover all 4096 positions; one record has exactly 2048 positions. record_starts[r] is the first position of record r, rising with r. segment_ids[t] is the record r with record_starts[r] <= t < record_starts[r] + record_lengths[r].
All inputs are finite; a program needn't handle non-finite values.
Results may differ from a plain program's by a relative error of at most 0.0005.
Values may be sent and summed in bfloat16 or wider, within the bound.
No kernel may reach another device: no remote copies, remote signals or barrier semaphores. Data moves between devices by JAX's collectives and lax.ppermute only.
A program may use at most 64 MiB of HBM per device.

v0:
```python
import functools

import jax
import jax.numpy as jnp
from jax import lax
from jax.experimental import pallas as pl
from jax.experimental.pallas import tpu as pltpu
from jax.sharding import Mesh
from jax.sharding import PartitionSpec as P

D = 8192
HEAD_DIM = 128
GROUP = 4
MASKED = -1e30
SCALE = HEAD_DIM**-0.5 * 1.4426950408889634
POSITIONS = ("z", "core")
CHIPS = 16
LONG = 2048
SMEM = pl.BlockSpec(memory_space=pltpu.SMEM)
VMEM = pl.BlockSpec(memory_space=pltpu.VMEM)


def cost(nanoseconds):
    return pl.CostEstimate(flops=nanoseconds * 1_000_000, bytes_accessed=1 << 20, transcendentals=0)


def as_line(scalars):
    lane = lax.broadcasted_iota(jnp.int32, (1, HEAD_DIM), 1)
    line = jnp.zeros((1, HEAD_DIM), jnp.int32)
    for record in range(scalars.shape[0]):
        line = jnp.where(lane == record, scalars[record], line)
    return line


def pack_kernel(starts, lengths, x_ref, out_ref, lines_ref, chip_ref):
    for head in range(GROUP):
        for stream in range(3):
            out_ref[head, stream] = x_ref[stream, :, head * HEAD_DIM : (head + 1) * HEAD_DIM]
    long_start = jnp.int32(0)
    for record in range(starts.shape[0]):
        long_start = jnp.where(lengths[record] == LONG, starts[record], long_start)
    chip_ref[0] = long_start // (2 * x_ref.shape[1])
    lines_ref[0] = as_line(starts)
    lines_ref[1] = as_line(lengths)


def pack(starts, lengths, streams):
    rows = streams.shape[1]
    return pl.pallas_call(
        pack_kernel,
        out_shape=(
            jax.ShapeDtypeStruct((GROUP, 3, rows, HEAD_DIM), streams.dtype),
            jax.ShapeDtypeStruct((2, 1, HEAD_DIM), jnp.int32),
            jax.ShapeDtypeStruct((1,), jnp.int32),
        ),
        in_specs=[SMEM, SMEM, VMEM],
        out_specs=(VMEM, VMEM, SMEM),
        name="pack_heads",
    )(starts, lengths, streams)


def cut_of(long_chip):
    return (long_chip + 1) % GROUP, (long_chip + 1) // GROUP % 2


def group_of(cut):
    return lax.rem(lax.axis_index("z") + CHIPS - cut, CHIPS) // GROUP


def attend_rows(q, query_pos, row_start, sources, state):
    rows = q.shape[0]
    scores = []
    for keys, _, first in sources:
        s = lax.dot_general(q, keys, (((1,), (1,)), ((), ())), preferred_element_type=jnp.float32)
        key_pos = jnp.concatenate(
            [here + lax.broadcasted_iota(jnp.int32, (1, rows), 1) for here in first], axis=1
        )
        allowed = (key_pos >= row_start) & (key_pos <= query_pos)
        scores.append(jnp.where(allowed, s * SCALE, MASKED))
    top = functools.reduce(jnp.maximum, [jnp.max(s, axis=1, keepdims=True) for s in scores])
    if state is not None:
        top = jnp.maximum(top, state[0])
    total = jnp.zeros((rows, 1), jnp.float32)
    summed = jnp.zeros((rows, HEAD_DIM), jnp.float32)
    for s, (_, values, _) in zip(scores, sources):
        weights = jnp.exp2(s - top)
        total = total + jnp.sum(weights, axis=1, keepdims=True)
        summed = summed + jnp.dot(
            weights.astype(jnp.bfloat16), values, preferred_element_type=jnp.float32
        )
    if state is not None:
        factor = jnp.exp2(state[0] - top)
        total = total + state[1] * factor
        summed = summed + state[2] * factor
    return top, total, summed


def chip_position(cut, group, place, core, rows):
    chip = lax.rem(group * GROUP + place + (cut + 2 * CHIPS), CHIPS)
    return (chip * 2 + core) * rows


def blocks_of(ref, low, high, offset=0):
    rows = ref.shape[2]
    return [ref[low:high, offset + i].reshape((high - low) * rows, HEAD_DIM) for i in range(2)]


def attend_kernel(long_chip, phase, starts, q_ref, *refs):
    cut, even = cut_of(long_chip)
    group, core = group_of(cut), lax.axis_index("core")
    rows = q_ref.shape[2]
    place = lax.broadcasted_iota(jnp.int32, (rows, 1), 0)

    is_even = lax.rem(group + even, 2) == 0

    def own(ref, of_core, count, offset=0):
        blocks = blocks_of(ref, 0, count, offset)
        return *blocks, [chip_position(cut, group, i, of_core, rows) for i in range(count)]

    def before(ref, of_core):
        first = [chip_position(cut, group - 1, i, of_core, rows) for i in range(GROUP)]
        return *blocks_of(ref, 0, GROUP), [jnp.where(is_even, -2 * LONG, here) for here in first]

    def edge(ref, of_core):
        back = jnp.where(is_even, 1, 2)
        return ref[0, 0], ref[0, 1], [chip_position(cut, group - back, GROUP - 1, of_core, rows)]

    if phase == 0:
        other, *outs = refs
        sources = [own(q_ref, core, GROUP, 1), own(other, 1 - core, GROUP)]
    else:
        from_core = core if phase == 1 else 1 - core
        sources = [before(refs[0], from_core), edge(refs[1], from_core)]
        state, outs = refs[2:5], refs[5:]

    @pl.loop(0, GROUP)
    def _(block):
        query_pos = chip_position(cut, group, block, core, rows) + place
        top, total, summed = attend_rows(
            q_ref[block, 0],
            query_pos,
            row_starts(starts, query_pos),
            sources,
            None if phase == 0 else [ref[block] for ref in state],
        )
        if phase < 2:
            outs[0][block], outs[1][block], outs[2][block] = top, total, summed
        else:
            outs[0][block] = summed / total


def attend(long_chip, phase, starts, received, *others):
    rows = received.shape[2]
    column = jax.ShapeDtypeStruct((GROUP, rows, 1), jnp.float32)
    full = jax.ShapeDtypeStruct((GROUP, rows, HEAD_DIM), jnp.float32)
    return pl.pallas_call(
        functools.partial(attend_kernel, long_chip, phase),
        out_shape=full if phase == 2 else (column, column, full),
        in_specs=[SMEM] + [VMEM] * (1 + len(others)),
        compiler_params=pltpu.CompilerParams(vmem_limit_bytes=32 * 1024 * 1024),
        cost_estimate=cost(2000),
        name=f"attend{phase}",
    )(starts, received, *others)


def row_starts(starts, positions):
    found = jnp.zeros_like(positions)
    for record in range(starts.shape[0]):
        here = starts[record]
        found = jnp.where(positions >= here, here, found)
    return found


def hyena_kernel(starts, residual, streams, rim, taps_ref, out_ref, padded):
    rows = residual.shape[0]
    edge = rim.shape[1]
    taps = taps_ref.shape[0]
    positions = lax.axis_index(POSITIONS) * rows + lax.broadcasted_iota(jnp.int32, (rows, 1), 0)
    first = row_starts(starts, positions)
    padded[:edge] = rim[0].astype(jnp.float32) * rim[1].astype(jnp.float32)
    padded[edge:] = streams[1].astype(jnp.float32) * streams[2].astype(jnp.float32)
    filtered = jnp.zeros(out_ref.shape, jnp.float32)
    for tap in range(taps):
        term = taps_ref[tap : tap + 1, :] * padded[edge - tap : edge - tap + rows]
        filtered = filtered + jnp.where(positions - tap >= first, term, 0.0)
    out_ref[...] = residual[...].astype(jnp.float32) + streams[0].astype(jnp.float32) * filtered


def stream_kernel(base, heads, stream_ref, squares_ref):
    rows = base.shape[0]
    squares = jnp.zeros((rows, HEAD_DIM), jnp.float32)
    for head in range(GROUP):
        columns = slice(head * HEAD_DIM, (head + 1) * HEAD_DIM)
        value = base[:, columns] + heads[head]
        stream_ref[:, columns] = value
        squares = squares + value * value
    line = jnp.sum(squares.T, axis=0, keepdims=True)
    for device in range(squares_ref.shape[0]):
        squares_ref[device] = line


def records_kernel(lines, parts, mean_ref, sums_ref):
    rows = parts.shape[2]
    line = jnp.sum(parts[:, 0, :], axis=0, keepdims=True) / D
    mean = jnp.broadcast_to(line, (rows, rows)).T
    mean_ref[...] = mean
    position = lax.axis_index(POSITIONS) * rows + lax.broadcasted_iota(jnp.int32, (rows, rows), 0)
    first = lines[0]
    inside = (position >= first) & (position < first + lines[1])
    sums = jnp.sum(jnp.where(inside, mean, 0.0), axis=0, keepdims=True)
    for device in range(sums_ref.shape[0]):
        sums_ref[device] = sums


def scale_kernel(stream, mean, gain, out_ref):
    factor = lax.rsqrt(mean[...] + 1e-05)
    for head in range(GROUP):
        columns = slice(head * HEAD_DIM, (head + 1) * HEAD_DIM)
        out_ref[:, columns] = stream[:, columns] * factor * gain[:, columns]


def mixers(long_chip, packed, residual, streams, taps, starts):
    rows, width = residual.shape
    cut, even = cut_of(long_chip)
    seq = lax.axis_size(POSITIONS)
    groups = [
        [(cut + GROUP * k + i) % CHIPS for i in range(GROUP)] for k in range(CHIPS // GROUP)
    ]
    swap = [(0, 1), (1, 0)]

    def along(value, count, of_groups):
        pairs = [(i, (i + count * GROUP) % CHIPS) for k in of_groups for i in groups[k]]
        return lax.ppermute(value, "z", pairs)

    evens, odds = [even, even + 2], [1 - even, 3 - even]
    rim = lax.ppermute(streams[1:, rows - 16 :], POSITIONS, [(i, i + 1) for i in range(seq - 1)])
    received = lax.all_to_all(packed, "z", 0, 0, axis_index_groups=groups, tiled=True)
    key_value, rim = lax.optimization_barrier((received[:, 1:], rim))
    before = along(key_value, 1, evens)
    last = received[GROUP - 1 :, 1:]
    edge = along(last, 2, odds) + along(last, 1, odds)
    base = pl.pallas_call(
        hyena_kernel,
        out_shape=jax.ShapeDtypeStruct((rows, width), jnp.float32),
        in_specs=[SMEM, VMEM, VMEM, VMEM, VMEM],
        out_specs=VMEM,
        scratch_shapes=[pltpu.VMEM((rows + 16, width), jnp.float32)],
        cost_estimate=cost(2000),
        name="hyena",
    )(starts, residual, streams, rim, taps)
    key_value, base = lax.optimization_barrier((key_value, base))
    other = lax.ppermute(key_value, "core", swap)
    state = attend(long_chip, 0, starts, received, other)
    edge_other = lax.ppermute(edge, "core", swap)
    before, edge, edge_other, state = lax.optimization_barrier((before, edge, edge_other, state))
    before_other = lax.ppermute(before, "core", swap)
    state = attend(long_chip, 1, starts, received, before, edge, *state)
    out = attend(long_chip, 2, starts, received, before_other, edge_other, *state)
    out = out.astype(jnp.float16)
    heads = lax.all_to_all(out, "z", 0, 0, axis_index_groups=groups, tiled=True)
    return base, heads.astype(jnp.float32)


def on_device(
    residual,
    hyena_streams,
    hyena_filter,
    attention_streams,
    norm_gain,
    record_starts,
    record_lengths,
    segment_ids,
):
    rows, width = residual.shape
    records = record_starts.shape[0]
    seq, mp = lax.axis_size(POSITIONS), lax.axis_size("mp")
    packed, lines, chip = pack(record_starts, record_lengths, attention_streams.transpose(1, 0, 2))
    base, heads = lax.switch(
        chip[0],
        [functools.partial(mixers, here) for here in range(CHIPS - LONG // (2 * rows) + 1)],
        packed,
        residual,
        hyena_streams.transpose(1, 0, 2),
        hyena_filter,
        record_starts,
    )

    with jax.named_scope("mean_square"):
        stream, squares = pl.pallas_call(
            stream_kernel,
            out_shape=(
                jax.ShapeDtypeStruct((rows, width), jnp.float32),
                jax.ShapeDtypeStruct((mp, 1, rows), jnp.float32),
            ),
            name="stream",
        )(base, heads)
        parts = lax.all_to_all(squares, "mp", 0, 0, tiled=True)
    with jax.named_scope("record_energy"):
        mean, sums = pl.pallas_call(
            records_kernel,
            out_shape=(
                jax.ShapeDtypeStruct((rows, rows), jnp.float32),
                jax.ShapeDtypeStruct((seq, 1, 128), jnp.float32),
            ),
            name="records",
        )(lines, parts)
        sums = lax.all_to_all(sums, POSITIONS, 0, 0, tiled=True)
        record_energy = jnp.sum(sums, axis=(0, 1))[:records] / record_lengths.astype(jnp.float32)
    mixed = pl.pallas_call(
        scale_kernel,
        out_shape=jax.ShapeDtypeStruct((rows, width), jnp.float32),
        cost_estimate=cost(1000),
        name="scale",
    )(stream, mean, norm_gain[None, :])
    return (mixed, record_energy)


def solution(mesh):
    fine = Mesh(mesh.devices.reshape(CHIPS, 2, mesh.shape["mp"]), ("z", "core", "mp"))
    return jax.shard_map(
        on_device,
        mesh=fine,
        in_specs=(
            P(POSITIONS, "mp"),
            P(POSITIONS, None, "mp"),
            P(None, "mp"),
            P(POSITIONS, None, "mp"),
            P("mp"),
            P(),
            P(),
            P(POSITIONS),
        ),
        out_specs=(P(POSITIONS, "mp"), P()),
        check_vma=False,
    )
```

profile of v0, /device:TPU:1, one launch (start us, length us, event | category | flops | bytes accessed | tf_op | source)
XLA Modules:
  0.0 123.6 jit_solution(13356883676629397612)
XLA Ops:
  0.6 0.0 copy-start.1
  0.6 0.0 copy-start
  0.7 0.6 copy-done.1
  1.3 1.8 %pack_heads.1 = (bf16[4,3,128,128]{3,2,1,0:T(8,128)(2,1)}, s32[2,1,128]{2,1,0:T(1,128)}, s32[1]{0:T(128)}) custom-call(s32[16]{0:T(128)S(1)} %copy-done.1, s32[16]{0:T(128)} %lengths.1, bf16[3,128,512]{2,1,0:T(8,128)(2,1)} %bitcast.4), custom_call_target="tpu_custom_call" | custom-call | tf_op jit(solution)/shard_map/pack_heads/pallas_call | solution.py:49
  3.8 0.0 copy-done
  3.8 73.9 %conditional.4 = (f32[128,512]{1,0:T(8,128)S(1)}, f32[4,128,128]{2,1,0:T(8,128)S(1)}) conditional(s32[]{:T(128)} %bitcast.1, (bf16[4,3,128,128]{3,2,1,0:T(8,128)(2,1)}, bf16[3,128,512]{2,1,0:T(8,128)(2,1)S(1)}, s32[16]{0:T(128)S(1)}, bf16[128,512]{1,0:T(8,128)(2,1)}, f32[7,512]{1,0:T(8,128)}) %tuple.148, ...), branch_computations={%region_0.0_spmd, %region_1.0_spmd, %region_2.0_spmd, %region_3.0_... | conditional | flops 8000163840 | bytes 12116380
  4.0 14.4 %all-to-all-start.8 = ((bf16[4,3,128,128]{3,2,1,0:T(8,128)(2,1)}), bf16[4,3,128,128]{3,2,1,0:T(8,128)(2,1)S(1)}, u32[]{:S(2)}, u32[]{:S(2)}) async-start(bf16[4,3,128,128]{3,2,1,0:T(8,128)(2,1)} %get-tuple-element.182), calls=%async_computation.8 | async-start | bytes 786432 | tf_op jit(solution)/shard_map/cond/branch_4_fun/all_to_all | solution.py:237
  18.4 0.0 copy-start.7
  18.4 0.0 copy-start.25
  18.4 2.1 %collective-permute-start.28 = (bf16[2,16,512]{2,1,0:T(8,128)(2,1)S(1)}, bf16[2,16,512]{2,1,0:T(8,128)(2,1)S(1)}, u32[]{:S(2)}, u32[]{:S(2)}) collective-permute-start(bf16[2,16,512]{2,1,0:T(8,128)(2,1)S(1)} %slice.69), channel_id=1, source_target_pairs={{0,16},{16,32},{32,48},{48,64},{64,80},{80,96},{96,112},{112,128},... | collective-permute-start | bytes 98312 | tf_op jit(solution)/shard_map/cond/branch_4_fun/ppermute | solution.py:236
  20.5 6.7 %all-to-all-done.8.q_ref = bf16[4,3,128,128]{3,2,1,0:T(8,128)(2,1)S(1)} async-done(((bf16[4,3,128,128]{3,2,1,0:T(8,128)(2,1)}), bf16[4,3,128,128]{3,2,1,0:T(8,128)(2,1)S(1)}, u32[]{:S(2)}, u32[]{:S(2)}) %all-to-all-start.8) | async-done | bytes 393248 | tf_op jit(solution)/shard_map/cond/branch_4_fun/all_to_all | solution.py:237
  27.2 0.0 collective-permute-done.28.rim
  27.2 0.0 copy-start.16
  27.2 0.6 copy-done.16
  27.8 0.0 copy-done.7
  27.8 0.0 copy-done.25
  27.8 1.3 %hyena.13 = f32[128,512]{1,0:T(8,128)S(1)} custom-call(s32[16]{0:T(128)S(1)} %get-tuple-element.185.starts, bf16[128,512]{1,0:T(8,128)(2,1)S(1)} %copy-done.7, bf16[3,128,512]{2,1,0:T(8,128)(2,1)S(1)} %get-tuple-element.183.streams, bf16[2,16,512]{2,1,0:T(8,128)(2,1)} %copy-done.16, f32[7,512]{1,0:T(8,128)S(1)} %copy-done.25), custom_call_target="tpu_custom_call" | custom-call | flops 2000000000 | bytes 1048576 | tf_op jit(solution)/shard_map/cond/branch_4_fun/hyena/pallas_call | solution.py:242
  29.1 4.0 %collective-permute-start.33 = (bf16[4,2,128,128]{3,2,1,0:T(8,128)(2,1)S(1)}, bf16[4,2,128,128]{3,2,1,0:T(8,128)(2,1)S(1)}, u32[]{:S(2)}, u32[]{:S(2)}) collective-permute-start(bf16[4,2,128,128]{3,2,1,0:T(8,128)(2,1)S(1)} %slice.93), channel_id=1, source_target_pairs={{0,16},{16,0},{1,17},{17,1},{2,18},{18,2},{3,19},{19,3},{4,20},{20... | collective-permute-start | bytes 786440 | tf_op jit(solution)/shard_map/cond/branch_4_fun/ppermute | solution.py:252
  33.2 1.3 %collective-permute-start.29 = (bf16[4,2,128,128]{3,2,1,0:T(8,128)(2,1)S(1)}, bf16[4,2,128,128]{3,2,1,0:T(8,128)(2,1)S(1)}, u32[]{:S(2)}, u32[]{:S(2)}) collective-permute-start(bf16[4,2,128,128]{3,2,1,0:T(8,128)(2,1)S(1)} %slice.93), channel_id=1, source_target_pairs={{160,288},{192,320},{224,352},{256,384},{416,32},{448,64},{480,96}... | collective-permute-start | bytes 786440 | tf_op jit(solution)/shard_map/cond/branch_4_fun/ppermute | solution.py:233
  34.5 0.7 collective-permute-start.30
  35.2 1.3 %collective-permute-start.31 = (bf16[1,2,128,128]{3,2,1,0:T(8,128)(2,1)S(1)}, bf16[1,2,128,128]{3,2,1,0:T(8,128)(2,1)S(1)}, u32[]{:S(2)}, u32[]{:S(2)}) collective-permute-start(bf16[1,2,128,128]{3,2,1,0:T(8,128)(2,1)S(1)} %slice.94), channel_id=1, source_target_pairs={{32,160},{64,192},{96,224},{128,256},{288,416},{320,448},{352,480}... | collective-permute-start | bytes 196616 | tf_op jit(solution)/shard_map/cond/branch_4_fun/ppermute | solution.py:233
  36.5 0.0 collective-permute-done.30
  36.5 13.4 %collective-permute-done.31 = bf16[1,2,128,128]{3,2,1,0:T(8,128)(2,1)S(1)} collective-permute-done((bf16[1,2,128,128]{3,2,1,0:T(8,128)(2,1)S(1)}, bf16[1,2,128,128]{3,2,1,0:T(8,128)(2,1)S(1)}, u32[]{:S(2)}, u32[]{:S(2)}) %collective-permute-start.31) | collective-permute-done | bytes 65568 | tf_op jit(solution)/shard_map/cond/branch_4_fun/ppermute | solution.py:233
  49.9 2.8 %collective-permute-start.32 = (bf16[1,2,128,128]{3,2,1,0:T(8,128)(2,1)S(1)}, bf16[1,2,128,128]{3,2,1,0:T(8,128)(2,1)S(1)}, u32[]{:S(2)}, u32[]{:S(2)}) collective-permute-start(bf16[1,2,128,128]{3,2,1,0:T(8,128)(2,1)S(1)} %add.22.refs_1_), channel_id=1, source_target_pairs={{0,16},{16,0},{1,17},{17,1},{2,18},{18,2},{3,19},{19,3},{4,20},{20... | collective-permute-start | bytes 196616 | tf_op jit(solution)/shard_map/cond/branch_4_fun/ppermute | solution.py:254
  52.8 0.0 collective-permute-done.33.refs_0_
  52.8 2.8 %attend0.13 = (f32[4,128,1]{2,1,0:T(8,128)S(1)}, f32[4,128,1]{2,1,0:T(8,128)S(1)}, f32[4,128,128]{2,1,0:T(8,128)S(1)}) custom-call(s32[16]{0:T(128)S(1)} %get-tuple-element.185.starts, bf16[4,3,128,128]{3,2,1,0:T(8,128)(2,1)S(1)} %all-to-all-done.8.q_ref, bf16[4,2,128,128]{3,2,1,0:T(8,128)(2,1)S(1)} %collective-permute-done.33.refs_0_), custom_call_target="tpu_custom_call" | custom-call | flops 2000000000 | bytes 1048576 | tf_op jit(solution)/shard_map/cond/branch_4_fun/attend0/pallas_call | solution.py:156
  55.6 0.0 collective-permute-done.32.refs_1_
  55.6 3.9 %collective-permute-done.29.refs_0_ = bf16[4,2,128,128]{3,2,1,0:T(8,128)(2,1)S(1)} collective-permute-done((bf16[4,2,128,128]{3,2,1,0:T(8,128)(2,1)S(1)}, bf16[4,2,128,128]{3,2,1,0:T(8,128)(2,1)S(1)}, u32[]{:S(2)}, u32[]{:S(2)}) %collective-permute-start.29) | collective-permute-done | bytes 262176 | tf_op jit(solution)/shard_map/cond/branch_4_fun/ppermute | solution.py:233
  59.5 2.3 %collective-permute-start.34 = (bf16[4,2,128,128]{3,2,1,0:T(8,128)(2,1)S(1)}, bf16[4,2,128,128]{3,2,1,0:T(8,128)(2,1)S(1)}, u32[]{:S(2)}, u32[]{:S(2)}) collective-permute-start(bf16[4,2,128,128]{3,2,1,0:T(8,128)(2,1)S(1)} %collective-permute-done.29.refs_0_), channel_id=1, source_target_pairs={{0,16},{16,0},{1,17},{17,1},{2,18},{18,2},{3,19},{19,3},{4,20},{20... | collective-permute-start | bytes 786440 | tf_op jit(solution)/shard_map/cond/branch_4_fun/ppermute | solution.py:256
  61.8 3.0 %attend1.13 = (f32[4,128,1]{2,1,0:T(8,128)S(1)}, f32[4,128,1]{2,1,0:T(8,128)S(1)}, f32[4,128,128]{2,1,0:T(8,128)S(1)}) custom-call(s32[16]{0:T(128)S(1)} %get-tuple-element.185.starts, bf16[4,3,128,128]{3,2,1,0:T(8,128)(2,1)S(1)} %all-to-all-done.8.q_ref, bf16[4,2,128,128]{3,2,1,0:T(8,128)(2,1)S(1)} %collective-permute-done.29.refs_0_, ...), custom_call_target="tpu_custom_call" | custom-call | flops 2000000000 | bytes 1048576 | tf_op jit(solution)/shard_map/cond/branch_4_fun/attend1/pallas_call | solution.py:156
  64.8 0.0 collective-permute-done.34.refs_0_
  64.8 3.1 %attend2.13 = f32[4,128,128]{2,1,0:T(8,128)S(1)} custom-call(s32[16]{0:T(128)S(1)} %get-tuple-element.185.starts, bf16[4,3,128,128]{3,2,1,0:T(8,128)(2,1)S(1)} %all-to-all-done.8.q_ref, bf16[4,2,128,128]{3,2,1,0:T(8,128)(2,1)S(1)} %collective-permute-done.34.refs_0_, bf16[1,2,128,128]{3,2,1,0:T(8,128)(2,1)S(1)} %collective-permute-done.32.refs_1_, ...), custom_call_target="tpu_custom_call" | custom-call | flops 2000000000 | bytes 1048576 | tf_op jit(solution)/shard_map/cond/branch_4_fun/attend2/pallas_call | solution.py:156
  68.0 9.4 %all_to_all.86 = f16[4,128,128]{2,1,0:T(8,128)(2,1)S(1)} all-to-all(f16[4,128,128]{2,1,0:T(8,128)(2,1)S(1)} %convert_element_type.66), channel_id=1, replica_groups={{32,64,96,128},{160,192,224,256},{288,320,352,384},{416,448,480,0},{33,..., dimensions={0} | all-to-all | bytes 262144 | tf_op jit(solution)/shard_map/cond/branch_4_fun/all_to_all | solution.py:260
  77.7 0.7 stream.1
  78.4 13.2 %all_to_all.91.parts = f32[16,1,128]{2,1,0:T(1,128)} all-to-all(f32[16,1,128]{2,1,0:T(1,128)} %get-tuple-element.304), channel_id=1, replica_groups=mesh['z'=16,'core'=2,'mp'=16] {'mp'}, dimensions={0} | all-to-all | bytes 16384 | tf_op jit(solution)/shard_map/mean_square/all_to_all | solution.py:297
  91.6 1.4 %records.1 = (f32[128,128]{1,0:T(8,128)}, f32[32,1,128]{2,1,0:T(1,128)}) custom-call(s32[2,1,128]{2,1,0:T(1,128)} %get-tuple-element.303.lines, f32[16,1,128]{2,1,0:T(1,128)} %all_to_all.91.parts), custom_call_target="tpu_custom_call" | custom-call | tf_op jit(solution)/shard_map/record_energy/records/pallas_call | solution.py:299
  93.1 18.1 %all-to-all-start.19 = ((f32[32,1,128]{2,1,0:T(1,128)}), f32[32,1,128]{2,1,0:T(1,128)S(1)}, u32[]{:S(2)}, u32[]{:S(2)}) async-start(f32[32,1,128]{2,1,0:T(1,128)} %get-tuple-element.306), calls=%async_computation.19 | async-start | bytes 32768 | tf_op jit(solution)/shard_map/record_energy/all_to_all | solution.py:307
  111.2 1.7 %scale.1 = f32[128,512]{1,0:T(8,128)} custom-call(f32[128,512]{1,0:T(8,128)} %get-tuple-element.302.stream, f32[128,128]{1,0:T(8,128)} %get-tuple-element.305.mean, f32[1,512]{1,0:T(1,128)} %bitcast.14), custom_call_target="tpu_custom_call" | custom-call | flops 1000000000 | bytes 1048576 | tf_op jit(solution)/shard_map/scale/pallas_call | solution.py:309
  112.9 0.0 copy-start.2
  112.9 10.1 %all-to-all-done.19 = f32[32,1,128]{2,1,0:T(1,128)S(1)} async-done(((f32[32,1,128]{2,1,0:T(1,128)}), f32[32,1,128]{2,1,0:T(1,128)S(1)}, u32[]{:S(2)}, u32[]{:S(2)}) %all-to-all-start.19) | async-done | bytes 16416 | tf_op jit(solution)/shard_map/record_energy/all_to_all | solution.py:307
  123.0 0.1 reduce_sum.9
  123.0 0.0 copy-done.2
  123.0 0.5 convert_divide_fusion
  (6 shorter events, 0.1 us)
Async XLA Ops:
  0.6 0.7 copy-start.1
  0.6 3.1 %copy-start = (bf16[128,3,512]{2,0,1:T(8,128)(2,1)S(1)}, bf16[128,3,512]{2,0,1:T(8,128)(2,1)}, u32[]{:S(2)}) copy-start(bf16[128,3,512]{2,0,1:T(8,128)(2,1)} %param.18) | copy-start | bytes 1179652
  4.0 23.1 %all-to-all-start.8 = ((bf16[4,3,128,128]{3,2,1,0:T(8,128)(2,1)}), bf16[4,3,128,128]{3,2,1,0:T(8,128)(2,1)S(1)}, u32[]{:S(2)}, u32[]{:S(2)}) async-start(bf16[4,3,128,128]{3,2,1,0:T(8,128)(2,1)} %get-tuple-element.182), calls=%async_computation.8 | async-start | bytes 786432 | tf_op jit(solution)/shard_map/cond/branch_4_fun/all_to_all | solution.py:237
  18.4 9.4 %copy-start.7 = (bf16[128,512]{1,0:T(8,128)(2,1)S(1)}, bf16[128,512]{1,0:T(8,128)(2,1)}, u32[]{:S(2)}) copy-start(bf16[128,512]{1,0:T(8,128)(2,1)} %get-tuple-element.186.residual) | copy-start | bytes 393220
  18.4 9.4 %copy-start.25 = (f32[7,512]{1,0:T(8,128)S(1)}, f32[7,512]{1,0:T(8,128)}, u32[]{:S(2)}) copy-start(f32[7,512]{1,0:T(8,128)} %get-tuple-element.188.taps_ref) | copy-start | bytes 43012
  18.4 8.8 %collective-permute-start.28 = (bf16[2,16,512]{2,1,0:T(8,128)(2,1)S(1)}, bf16[2,16,512]{2,1,0:T(8,128)(2,1)S(1)}, u32[]{:S(2)}, u32[]{:S(2)}) collective-permute-start(bf16[2,16,512]{2,1,0:T(8,128)(2,1)S(1)} %slice.69), channel_id=1, source_target_pairs={{0,16},{16,32},{32,48},{48,64},{64,80},{80,96},{96,112},{112,128},... | collective-permute-start | bytes 98312 | tf_op jit(solution)/shard_map/cond/branch_4_fun/ppermute | solution.py:236
  27.2 0.6 copy-start.16
  29.1 23.6 %collective-permute-start.33 = (bf16[4,2,128,128]{3,2,1,0:T(8,128)(2,1)S(1)}, bf16[4,2,128,128]{3,2,1,0:T(8,128)(2,1)S(1)}, u32[]{:S(2)}, u32[]{:S(2)}) collective-permute-start(bf16[4,2,128,128]{3,2,1,0:T(8,128)(2,1)S(1)} %slice.93), channel_id=1, source_target_pairs={{0,16},{16,0},{1,17},{17,1},{2,18},{18,2},{3,19},{19,3},{4,20},{20... | collective-permute-start | bytes 786440 | tf_op jit(solution)/shard_map/cond/branch_4_fun/ppermute | solution.py:252
  33.2 26.3 %collective-permute-start.29 = (bf16[4,2,128,128]{3,2,1,0:T(8,128)(2,1)S(1)}, bf16[4,2,128,128]{3,2,1,0:T(8,128)(2,1)S(1)}, u32[]{:S(2)}, u32[]{:S(2)}) collective-permute-start(bf16[4,2,128,128]{3,2,1,0:T(8,128)(2,1)S(1)} %slice.93), channel_id=1, source_target_pairs={{160,288},{192,320},{224,352},{256,384},{416,32},{448,64},{480,96}... | collective-permute-start | bytes 786440 | tf_op jit(solution)/shard_map/cond/branch_4_fun/ppermute | solution.py:233
  34.5 2.0 %collective-permute-start.30 = (bf16[1,2,128,128]{3,2,1,0:T(8,128)(2,1)S(1)}, bf16[1,2,128,128]{3,2,1,0:T(8,128)(2,1)S(1)}, u32[]{:S(2)}, u32[]{:S(2)}) collective-permute-start(bf16[1,2,128,128]{3,2,1,0:T(8,128)(2,1)S(1)} %slice.94), channel_id=1, source_target_pairs={{32,288},{64,320},{96,352},{128,384},{288,32},{320,64},{352,96},{3... | collective-permute-start | bytes 196616 | tf_op jit(solution)/shard_map/cond/branch_4_fun/ppermute | solution.py:233
  35.2 14.7 %collective-permute-start.31 = (bf16[1,2,128,128]{3,2,1,0:T(8,128)(2,1)S(1)}, bf16[1,2,128,128]{3,2,1,0:T(8,128)(2,1)S(1)}, u32[]{:S(2)}, u32[]{:S(2)}) collective-permute-start(bf16[1,2,128,128]{3,2,1,0:T(8,128)(2,1)S(1)} %slice.94), channel_id=1, source_target_pairs={{32,160},{64,192},{96,224},{128,256},{288,416},{320,448},{352,480}... | collective-permute-start | bytes 196616 | tf_op jit(solution)/shard_map/cond/branch_4_fun/ppermute | solution.py:233
  49.9 5.7 %collective-permute-start.32 = (bf16[1,2,128,128]{3,2,1,0:T(8,128)(2,1)S(1)}, bf16[1,2,128,128]{3,2,1,0:T(8,128)(2,1)S(1)}, u32[]{:S(2)}, u32[]{:S(2)}) collective-permute-start(bf16[1,2,128,128]{3,2,1,0:T(8,128)(2,1)S(1)} %add.22.refs_1_), channel_id=1, source_target_pairs={{0,16},{16,0},{1,17},{17,1},{2,18},{18,2},{3,19},{19,3},{4,20},{20... | collective-permute-start | bytes 196616 | tf_op jit(solution)/shard_map/cond/branch_4_fun/ppermute | solution.py:254
  59.5 5.3 %collective-permute-start.34 = (bf16[4,2,128,128]{3,2,1,0:T(8,128)(2,1)S(1)}, bf16[4,2,128,128]{3,2,1,0:T(8,128)(2,1)S(1)}, u32[]{:S(2)}, u32[]{:S(2)}) collective-permute-start(bf16[4,2,128,128]{3,2,1,0:T(8,128)(2,1)S(1)} %collective-permute-done.29.refs_0_), channel_id=1, source_target_pairs={{0,16},{16,0},{1,17},{17,1},{2,18},{18,2},{3,19},{19,3},{4,20},{20... | collective-permute-start | bytes 786440 | tf_op jit(solution)/shard_map/cond/branch_4_fun/ppermute | solution.py:256
  93.1 29.9 %all-to-all-start.19 = ((f32[32,1,128]{2,1,0:T(1,128)}), f32[32,1,128]{2,1,0:T(1,128)S(1)}, u32[]{:S(2)}, u32[]{:S(2)}) async-start(f32[32,1,128]{2,1,0:T(1,128)} %get-tuple-element.306), calls=%async_computation.19 | async-start | bytes 32768 | tf_op jit(solution)/shard_map/record_energy/all_to_all | solution.py:307
  112.9 10.1 %copy-start.2 = (s32[16]{0:T(128)S(1)}, s32[16]{0:T(128)}, u32[]{:S(2)}) copy-start(s32[16]{0:T(128)} %lengths.1) | copy-start | bytes 196
where the time goes:
time: 124 us
  starting transfers between devices  46.9 us (38%)
  waiting for transfers between devices  34.1 us (28%)
  blocking collectives  22.6 us (18%)
  Pallas kernels  16 us (13%)
  between operations  1.33 us (1%)
  local copies, waits for them, and re-layouts  1.29 us (1%)
    all_to_all x1, starting transfers between devices, on_device(): sums = lax.all_to_all(sums, POSITIONS, 0, 0, tiled=True)  18.1 us
    ppermute x3, waiting for transfers between devices, along(): return lax.ppermute(value, 'z', pairs)  17.3 us
    all_to_all x1, starting transfers between devices, mixers(): lax.all_to_all(packed, 'z', 0, 0, axis_index_groups=groups, tiled=True)  14.4 us
    all_to_all x1, blocking collectives, on_device(): parts = lax.all_to_all(squares, 'mp', 0, 0, tiled=True)  13.2 us
    all_to_all x1, waiting for transfers between devices, on_device(): sums = lax.all_to_all(sums, POSITIONS, 0, 0, tiled=True)  10.1 us
    all_to_all x1, blocking collectives, mixers(): heads = lax.all_to_all(out, 'z', 0, 0, axis_index_groups=groups, tiled=True)  9.45 us
    pallas_call x3, Pallas kernels, attend(): pl.pallas_call(functools.partial(attend_kernel, long_chip, phase), out_sh...  8.92 us
    all_to_all x1, waiting for transfers between devices, mixers(): lax.all_to_all(packed, 'z', 0, 0, axis_index_groups=groups, tiled=True)  6.7 us
  transfers between devices with their start and end apart: 9, of which 4 were waited for; matrix products, arithmetic and copies ran while one was open for 0% of the time, Pallas kernels for 6%

commit v1 on v0

--- a/solution.py
+++ b/solution.py
@@ -67,7 +67,7 @@
     return lax.rem(lax.axis_index("z") + CHIPS - cut, CHIPS) // GROUP
 
 
-def attend_rows(q, query_pos, row_start, sources, state):
+def attend_rows(q, query_pos, row_start, sources, state, causal=True):
     rows = q.shape[0]
     scores = []
     for keys, _, first in sources:
@@ -75,7 +75,9 @@
         key_pos = jnp.concatenate(
             [here + lax.broadcasted_iota(jnp.int32, (1, rows), 1) for here in first], axis=1
         )
-        allowed = (key_pos >= row_start) & (key_pos <= query_pos)
+        allowed = key_pos >= row_start
+        if causal:
+            allowed = allowed & (key_pos <= query_pos)
         scores.append(jnp.where(allowed, s * SCALE, MASKED))
     top = functools.reduce(jnp.maximum, [jnp.max(s, axis=1, keepdims=True) for s in scores])
     if state is not None:
@@ -126,22 +128,29 @@
         return ref[0, 0], ref[0, 1], [chip_position(cut, group - back, GROUP - 1, of_core, rows)]
 
     if phase == 0:
-        other, *outs = refs
+        other, edge_ref, edge_other, *outs = refs
         sources = [own(q_ref, core, GROUP, 1), own(other, 1 - core, GROUP)]
+        sources += [edge(edge_ref, core), edge(edge_other, 1 - core)]
     else:
-        from_core = core if phase == 1 else 1 - core
-        sources = [before(refs[0], from_core), edge(refs[1], from_core)]
-        state, outs = refs[2:5], refs[5:]
+        sources = [before(refs[0], core if phase == 1 else 1 - core)]
+        state, outs = refs[1:4], refs[4:]
 
     @pl.loop(0, GROUP)
     def _(block):
-        query_pos = chip_position(cut, group, block, core, rows) + place
+        query_first = chip_position(cut, group, block, core, rows)
+        query_pos = query_first + place
+        here = sources
+        if phase > 0:
+            ((keys, values, firsts),) = sources
+            firsts = [jnp.where(first < query_first, first, -2 * LONG) for first in firsts]
+            here = [(keys, values, firsts)]
         top, total, summed = attend_rows(
             q_ref[block, 0],
             query_pos,
             row_starts(starts, query_pos),
-            sources,
+            here,
             None if phase == 0 else [ref[block] for ref in state],
+            causal=phase == 0,
         )
         if phase < 2:
             outs[0][block], outs[1][block], outs[2][block] = top, total, summed
@@ -158,7 +167,7 @@
         out_shape=full if phase == 2 else (column, column, full),
         in_specs=[SMEM] + [VMEM] * (1 + len(others)),
         compiler_params=pltpu.CompilerParams(vmem_limit_bytes=32 * 1024 * 1024),
-        cost_estimate=cost(2000),
+        cost_estimate=cost(2000 if phase else 10),
         name=f"attend{phase}",
     )(starts, received, *others)
 
@@ -238,6 +247,8 @@
     key_value, rim = lax.optimization_barrier((received[:, 1:], rim))
     before = along(key_value, 1, evens)
     last = received[GROUP - 1 :, 1:]
+    other = lax.ppermute(key_value, "core", swap)
+    last, streams, other = lax.optimization_barrier((last, streams, other))
     edge = along(last, 2, odds) + along(last, 1, odds)
     base = pl.pallas_call(
         hyena_kernel,
@@ -245,17 +256,15 @@
         in_specs=[SMEM, VMEM, VMEM, VMEM, VMEM],
         out_specs=VMEM,
         scratch_shapes=[pltpu.VMEM((rows + 16, width), jnp.float32)],
-        cost_estimate=cost(2000),
+        cost_estimate=cost(10),
         name="hyena",
     )(starts, residual, streams, rim, taps)
-    key_value, base = lax.optimization_barrier((key_value, base))
-    other = lax.ppermute(key_value, "core", swap)
-    state = attend(long_chip, 0, starts, received, other)
     edge_other = lax.ppermute(edge, "core", swap)
-    before, edge, edge_other, state = lax.optimization_barrier((before, edge, edge_other, state))
+    state = attend(long_chip, 0, starts, received, other, edge, edge_other)
+    before, state, base = lax.optimization_barrier((before, state, base))
     before_other = lax.ppermute(before, "core", swap)
-    state = attend(long_chip, 1, starts, received, before, edge, *state)
-    out = attend(long_chip, 2, starts, received, before_other, edge_other, *state)
+    state = attend(long_chip, 1, starts, received, before, *state)
+    out = attend(long_chip, 2, starts, received, before_other, *state)
     out = out.astype(jnp.float16)
     heads = lax.all_to_all(out, "z", 0, 0, axis_index_groups=groups, tiled=True)
     return base, heads.astype(jnp.float32)

time: 124 us -> 119 us (0.960)
  waiting for transfers between devices: 34.1 us -> 30.7 us
    all_to_all x1, starting transfers between devices: 18.1 us -> 9.78 us  [on_device(): sums = lax.all_to_all(sums, POSITIONS, 0, 0, tiled=True)]
    ppermute x3, starting transfers between devices: 3.26 us -> 10.7 us  [along(): return lax.ppermute(value, 'z', pairs)]
    ppermute x3, waiting for transfers between devices: 17.3 us -> 13.9 us  [along(): return lax.ppermute(value, 'z', pairs)]
  transfers between devices with their start and end apart: 9 -> 9, of which waited for: 4 -> 4; matrix products, arithmetic and copies ran while one was open for 0% -> 0% of each run, Pallas kernels for 6% -> 7%
where the time goes in v1:
time: 119 us
  starting transfers between devices  47.1 us (40%)
  waiting for transfers between devices  30.7 us (26%)
  blocking collectives  22.6 us (19%)
  Pallas kernels  15.5 us (13%)
  between operations  1.33 us (1%)
    all_to_all x1, starting transfers between devices, mixers(): lax.all_to_all(packed, 'z', 0, 0, axis_index_groups=groups, tiled=True)  14.4 us
    ppermute x3, waiting for transfers between devices, along(): return lax.ppermute(value, 'z', pairs)  13.9 us
    all_to_all x1, blocking collectives, on_device(): parts = lax.all_to_all(squares, 'mp', 0, 0, tiled=True)  13.2 us
    ppermute x3, starting transfers between devices, along(): return lax.ppermute(value, 'z', pairs)  10.7 us
    all_to_all x1, waiting for transfers between devices, on_device(): sums = lax.all_to_all(sums, POSITIONS, 0, 0, tiled=True)  10.1 us
    all_to_all x1, starting transfers between devices, on_device(): sums = lax.all_to_all(sums, POSITIONS, 0, 0, tiled=True)  9.78 us
    all_to_all x1, blocking collectives, mixers(): heads = lax.all_to_all(out, 'z', 0, 0, axis_index_groups=groups, tiled=True)  9.43 us
    pallas_call x3, Pallas kernels, attend(): pl.pallas_call(functools.partial(attend_kernel, long_chip, phase), out_sh...  8.41 us
  transfers between devices with their start and end apart: 9, of which 4 were waited for; matrix products, arithmetic and copies ran while one was open for 0% of the time, Pallas kernels for 7%

profile of v1, /device:TPU:1, one launch (start us, length us, event | category | flops | bytes accessed | tf_op | source)
XLA Modules:
  0.0 119.3 jit_solution(10716036839412566663)
XLA Ops:
  0.6 0.0 copy-start.19
  0.6 0.0 copy-start
  0.7 0.6 copy-done.19
  1.3 1.8 %pack_heads.1 = (bf16[4,3,128,128]{3,2,1,0:T(8,128)(2,1)}, s32[2,1,128]{2,1,0:T(1,128)}, s32[1]{0:T(128)}) custom-call(s32[16]{0:T(128)S(1)} %copy-done.19, s32[16]{0:T(128)} %lengths.1, bf16[3,128,512]{2,1,0:T(8,128)(2,1)} %bitcast.13), custom_call_target="tpu_custom_call" | custom-call | tf_op jit(solution)/shard_map/pack_heads/pallas_call | solution.py:49
  3.8 0.0 copy-done
  3.8 77.9 %conditional.4 = (f32[128,512]{1,0:T(8,128)S(1)}, f32[4,128,128]{2,1,0:T(8,128)S(1)}) conditional(s32[]{:T(128)} %bitcast.1, (bf16[4,3,128,128]{3,2,1,0:T(8,128)(2,1)}, bf16[3,128,512]{2,1,0:T(8,128)(2,1)S(1)}, s32[16]{0:T(128)S(1)}, bf16[128,512]{1,0:T(8,128)(2,1)}, f32[7,512]{1,0:T(8,128)}) %tuple.148, ...), branch_computations={%region_0.0_spmd, %region_1.0_spmd, %region_2.0_spmd, %region_3.0_... | conditional | flops 4020163840 | bytes 12116380
  4.0 14.4 %all-to-all-start.16 = ((bf16[4,3,128,128]{3,2,1,0:T(8,128)(2,1)}), bf16[4,3,128,128]{3,2,1,0:T(8,128)(2,1)S(1)}, u32[]{:S(2)}, u32[]{:S(2)}) async-start(bf16[4,3,128,128]{3,2,1,0:T(8,128)(2,1)} %get-tuple-element.266), calls=%async_computation.16 | async-start | bytes 786432 | tf_op jit(solution)/shard_map/cond/branch_8_fun/all_to_all | solution.py:246
  18.4 2.1 %collective-permute-start.56 = (bf16[2,16,512]{2,1,0:T(8,128)(2,1)S(1)}, bf16[2,16,512]{2,1,0:T(8,128)(2,1)S(1)}, u32[]{:S(2)}, u32[]{:S(2)}) collective-permute-start(bf16[2,16,512]{2,1,0:T(8,128)(2,1)S(1)} %slice.81), channel_id=1, source_target_pairs={{0,16},{16,32},{32,48},{48,64},{64,80},{80,96},{96,112},{112,128},... | collective-permute-start | bytes 98312 | tf_op jit(solution)/shard_map/cond/branch_8_fun/ppermute | solution.py:245
  20.6 6.6 %all-to-all-done.16.q_ref = bf16[4,3,128,128]{3,2,1,0:T(8,128)(2,1)S(1)} async-done(((bf16[4,3,128,128]{3,2,1,0:T(8,128)(2,1)}), bf16[4,3,128,128]{3,2,1,0:T(8,128)(2,1)S(1)}, u32[]{:S(2)}, u32[]{:S(2)}) %all-to-all-start.16) | async-done | bytes 393248 | tf_op jit(solution)/shard_map/cond/branch_8_fun/all_to_all | solution.py:246
  27.2 0.0 collective-permute-done.56.rim
  27.2 0.0 copy-start.28
  27.2 4.0 %collective-permute-start.58 = (bf16[4,2,128,128]{3,2,1,0:T(8,128)(2,1)S(1)}, bf16[4,2,128,128]{3,2,1,0:T(8,128)(2,1)S(1)}, u32[]{:S(2)}, u32[]{:S(2)}) collective-permute-start(bf16[4,2,128,128]{3,2,1,0:T(8,128)(2,1)S(1)} %slice.101), channel_id=1, source_target_pairs={{0,16},{16,0},{1,17},{17,1},{2,18},{18,2},{3,19},{19,3},{4,20},{20... | collective-permute-start | bytes 786440 | tf_op jit(solution)/shard_map/cond/branch_8_fun/ppermute | solution.py:250
  31.3 1.3 %collective-permute-start.57 = (bf16[4,2,128,128]{3,2,1,0:T(8,128)(2,1)S(1)}, bf16[4,2,128,128]{3,2,1,0:T(8,128)(2,1)S(1)}, u32[]{:S(2)}, u32[]{:S(2)}) collective-permute-start(bf16[4,2,128,128]{3,2,1,0:T(8,128)(2,1)S(1)} %slice.101), channel_id=1, source_target_pairs={{32,160},{64,192},{96,224},{128,256},{288,416},{320,448},{352,480}... | collective-permute-start | bytes 786440 | tf_op jit(solution)/shard_map/cond/branch_8_fun/ppermute | solution.py:242
  32.6 0.0 copy-done.28
  32.6 0.0 copy-start.9
  32.6 0.0 collective-permute-done.58.refs_0_
  32.6 7.8 %collective-permute-start.59 = (bf16[1,2,128,128]{3,2,1,0:T(8,128)(2,1)S(1)}, bf16[1,2,128,128]{3,2,1,0:T(8,128)(2,1)S(1)}, u32[]{:S(2)}, u32[]{:S(2)}) collective-permute-start(bf16[1,2,128,128]{3,2,1,0:T(8,128)(2,1)S(1)} %slice.102), channel_id=1, source_target_pairs={{160,416},{192,448},{224,480},{256,0},{416,160},{448,192},{480,224... | collective-permute-start | bytes 196616 | tf_op jit(solution)/shard_map/cond/branch_8_fun/ppermute | solution.py:242
  40.4 1.6 %collective-permute-start.60 = (bf16[1,2,128,128]{3,2,1,0:T(8,128)(2,1)S(1)}, bf16[1,2,128,128]{3,2,1,0:T(8,128)(2,1)S(1)}, u32[]{:S(2)}, u32[]{:S(2)}) collective-permute-start(bf16[1,2,128,128]{3,2,1,0:T(8,128)(2,1)S(1)} %slice.102), channel_id=1, source_target_pairs={{160,288},{192,320},{224,352},{256,384},{416,32},{448,64},{480,96}... | collective-permute-start | bytes 196616 | tf_op jit(solution)/shard_map/cond/branch_8_fun/ppermute | solution.py:242
  42.0 10.1 %collective-permute-done.59 = bf16[1,2,128,128]{3,2,1,0:T(8,128)(2,1)S(1)} collective-permute-done((bf16[1,2,128,128]{3,2,1,0:T(8,128)(2,1)S(1)}, bf16[1,2,128,128]{3,2,1,0:T(8,128)(2,1)S(1)}, u32[]{:S(2)}, u32[]{:S(2)}) %collective-permute-start.59) | collective-permute-done | bytes 65568 | tf_op jit(solution)/shard_map/cond/branch_8_fun/ppermute | solution.py:242
  52.1 0.0 collective-permute-done.60
  52.1 0.0 copy-start.18
  52.1 3.8 %collective-permute-start.61 = (bf16[1,2,128,128]{3,2,1,0:T(8,128)(2,1)S(1)}, bf16[1,2,128,128]{3,2,1,0:T(8,128)(2,1)S(1)}, u32[]{:S(2)}, u32[]{:S(2)}) collective-permute-start(bf16[1,2,128,128]{3,2,1,0:T(8,128)(2,1)S(1)} %add.26.refs_1_), channel_id=1, source_target_pairs={{0,16},{16,0},{1,17},{17,1},{2,18},{18,2},{3,19},{19,3},{4,20},{20... | collective-permute-start | bytes 196616 | tf_op jit(solution)/shard_map/cond/branch_8_fun/ppermute | solution.py:262
  55.9 0.0 copy-done.9
  56.0 0.0 copy-done.18
  56.0 1.3 %hyena.17 = f32[128,512]{1,0:T(8,128)S(1)} custom-call(s32[16]{0:T(128)S(1)} %get-tuple-element.269.starts, bf16[128,512]{1,0:T(8,128)(2,1)S(1)} %copy-done.9, bf16[3,128,512]{2,1,0:T(8,128)(2,1)S(1)} %get-tuple-element.276.streams, bf16[2,16,512]{2,1,0:T(8,128)(2,1)} %copy-done.28, f32[7,512]{1,0:T(8,128)S(1)} %copy-done.18), custom_call_target="tpu_custom_call" | custom-call | flops 10000000 | bytes 1048576 | tf_op jit(solution)/shard_map/cond/branch_8_fun/hyena/pallas_call | solution.py:253
  57.3 0.0 collective-permute-done.61.refs_2_
  57.3 3.1 %attend0.17 = (f32[4,128,1]{2,1,0:T(8,128)S(1)}, f32[4,128,1]{2,1,0:T(8,128)S(1)}, f32[4,128,128]{2,1,0:T(8,128)S(1)}) custom-call(s32[16]{0:T(128)S(1)} %get-tuple-element.269.starts, bf16[4,3,128,128]{3,2,1,0:T(8,128)(2,1)S(1)} %all-to-all-done.16.q_ref, bf16[4,2,128,128]{3,2,1,0:T(8,128)(2,1)S(1)} %collective-permute-done.58.refs_0_, ...), custom_call_target="tpu_custom_call" | custom-call | flops 10000000 | bytes 1048576 | tf_op jit(solution)/shard_map/cond/branch_8_fun/attend0/pallas_call | solution.py:165
  60.4 3.9 %collective-permute-done.57.refs_0_ = bf16[4,2,128,128]{3,2,1,0:T(8,128)(2,1)S(1)} collective-permute-done((bf16[4,2,128,128]{3,2,1,0:T(8,128)(2,1)S(1)}, bf16[4,2,128,128]{3,2,1,0:T(8,128)(2,1)S(1)}, u32[]{:S(2)}, u32[]{:S(2)}) %collective-permute-start.57) | collective-permute-done | bytes 262176 | tf_op jit(solution)/shard_map/cond/branch_8_fun/ppermute | solution.py:242
  64.2 2.3 %collective-permute-start.62 = (bf16[4,2,128,128]{3,2,1,0:T(8,128)(2,1)S(1)}, bf16[4,2,128,128]{3,2,1,0:T(8,128)(2,1)S(1)}, u32[]{:S(2)}, u32[]{:S(2)}) collective-permute-start(bf16[4,2,128,128]{3,2,1,0:T(8,128)(2,1)S(1)} %collective-permute-done.57.refs_0_), channel_id=1, source_target_pairs={{0,16},{16,0},{1,17},{17,1},{2,18},{18,2},{3,19},{19,3},{4,20},{20... | collective-permute-start | bytes 786440 | tf_op jit(solution)/shard_map/cond/branch_8_fun/ppermute | solution.py:265
  66.6 2.6 %attend1.17 = (f32[4,128,1]{2,1,0:T(8,128)S(1)}, f32[4,128,1]{2,1,0:T(8,128)S(1)}, f32[4,128,128]{2,1,0:T(8,128)S(1)}) custom-call(s32[16]{0:T(128)S(1)} %get-tuple-element.269.starts, bf16[4,3,128,128]{3,2,1,0:T(8,128)(2,1)S(1)} %all-to-all-done.16.q_ref, bf16[4,2,128,128]{3,2,1,0:T(8,128)(2,1)S(1)} %collective-permute-done.57.refs_0_, ...), custom_call_target="tpu_custom_call" | custom-call | flops 2000000000 | bytes 1048576 | tf_op jit(solution)/shard_map/cond/branch_8_fun/attend1/pallas_call | solution.py:165
  69.2 0.0 collective-permute-done.62.refs_0_
  69.2 2.8 %attend2.17 = f32[4,128,128]{2,1,0:T(8,128)S(1)} custom-call(s32[16]{0:T(128)S(1)} %get-tuple-element.269.starts, bf16[4,3,128,128]{3,2,1,0:T(8,128)(2,1)S(1)} %all-to-all-done.16.q_ref, bf16[4,2,128,128]{3,2,1,0:T(8,128)(2,1)S(1)} %collective-permute-done.62.refs_0_, f32[4,128,1]{2,1,0:T(8,128)S(1)} %get-tuple-element.284.refs_1_, ...), custom_call_target="tpu_custom_call" | custom-call | flops 2000000000 | bytes 1048576 | tf_op jit(solution)/shard_map/cond/branch_8_fun/attend2/pallas_call | solution.py:165
  72.0 9.4 %all_to_all.90 = f16[4,128,128]{2,1,0:T(8,128)(2,1)S(1)} all-to-all(f16[4,128,128]{2,1,0:T(8,128)(2,1)S(1)} %convert_element_type.74), channel_id=1, replica_groups={{32,64,96,128},{160,192,224,256},{288,320,352,384},{416,448,480,0},{33,..., dimensions={0} | all-to-all | bytes 262144 | tf_op jit(solution)/shard_map/cond/branch_8_fun/all_to_all | solution.py:269
  81.7 0.7 stream.1
  82.4 13.2 %all_to_all.91.parts = f32[16,1,128]{2,1,0:T(1,128)} all-to-all(f32[16,1,128]{2,1,0:T(1,128)} %get-tuple-element.304), channel_id=1, replica_groups=mesh['z'=16,'core'=2,'mp'=16] {'mp'}, dimensions={0} | all-to-all | bytes 16384 | tf_op jit(solution)/shard_map/mean_square/all_to_all | solution.py:306
  95.6 1.4 %records.1 = (f32[128,128]{1,0:T(8,128)}, f32[32,1,128]{2,1,0:T(1,128)}) custom-call(s32[2,1,128]{2,1,0:T(1,128)} %get-tuple-element.303.lines, f32[16,1,128]{2,1,0:T(1,128)} %all_to_all.91.parts), custom_call_target="tpu_custom_call" | custom-call | tf_op jit(solution)/shard_map/record_energy/records/pallas_call | solution.py:308
  97.1 9.8 %all-to-all-start.19 = ((f32[32,1,128]{2,1,0:T(1,128)}), f32[32,1,128]{2,1,0:T(1,128)S(1)}, u32[]{:S(2)}, u32[]{:S(2)}) async-start(f32[32,1,128]{2,1,0:T(1,128)} %get-tuple-element.306), calls=%async_computation.19 | async-start | bytes 32768 | tf_op jit(solution)/shard_map/record_energy/all_to_all | solution.py:316
  106.9 1.7 %scale.1 = f32[128,512]{1,0:T(8,128)} custom-call(f32[128,512]{1,0:T(8,128)} %get-tuple-element.302.stream, f32[128,128]{1,0:T(8,128)} %get-tuple-element.305.mean, f32[1,512]{1,0:T(1,128)} %bitcast.14), custom_call_target="tpu_custom_call" | custom-call | flops 1000000000 | bytes 1048576 | tf_op jit(solution)/shard_map/scale/pallas_call | solution.py:318
  108.6 0.0 copy-start.29
  108.6 10.1 %all-to-all-done.19 = f32[32,1,128]{2,1,0:T(1,128)S(1)} async-done(((f32[32,1,128]{2,1,0:T(1,128)}), f32[32,1,128]{2,1,0:T(1,128)S(1)}, u32[]{:S(2)}, u32[]{:S(2)}) %all-to-all-start.19) | async-done | bytes 16416 | tf_op jit(solution)/shard_map/record_energy/all_to_all | solution.py:316
  118.7 0.1 reduce_sum.9
  118.7 0.0 copy-done.29
  118.7 0.5 convert_divide_fusion
  (6 shorter events, 0.1 us)
Async XLA Ops:
  0.6 0.7 copy-start.19
  0.6 3.1 %copy-start = (bf16[128,3,512]{2,0,1:T(8,128)(2,1)S(1)}, bf16[128,3,512]{2,0,1:T(8,128)(2,1)}, u32[]{:S(2)}) copy-start(bf16[128,3,512]{2,0,1:T(8,128)(2,1)} %param.18) | copy-start | bytes 1179652
  4.0 23.1 %all-to-all-start.16 = ((bf16[4,3,128,128]{3,2,1,0:T(8,128)(2,1)}), bf16[4,3,128,128]{3,2,1,0:T(8,128)(2,1)S(1)}, u32[]{:S(2)}, u32[]{:S(2)}) async-start(bf16[4,3,128,128]{3,2,1,0:T(8,128)(2,1)} %get-tuple-element.266), calls=%async_computation.16 | async-start | bytes 786432 | tf_op jit(solution)/shard_map/cond/branch_8_fun/all_to_all | solution.py:246
  18.4 8.8 %collective-permute-start.56 = (bf16[2,16,512]{2,1,0:T(8,128)(2,1)S(1)}, bf16[2,16,512]{2,1,0:T(8,128)(2,1)S(1)}, u32[]{:S(2)}, u32[]{:S(2)}) collective-permute-start(bf16[2,16,512]{2,1,0:T(8,128)(2,1)S(1)} %slice.81), channel_id=1, source_target_pairs={{0,16},{16,32},{32,48},{48,64},{64,80},{80,96},{96,112},{112,128},... | collective-permute-start | bytes 98312 | tf_op jit(solution)/shard_map/cond/branch_8_fun/ppermute | solution.py:245
  27.2 5.4 %copy-start.28 = (bf16[2,16,512]{2,1,0:T(8,128)(2,1)}, bf16[2,16,512]{2,1,0:T(8,128)(2,1)S(1)}, u32[]{:S(2)}) copy-start(bf16[2,16,512]{2,1,0:T(8,128)(2,1)S(1)} %collective-permute-done.56.rim) | copy-start | bytes 98308
  27.2 5.4 %collective-permute-start.58 = (bf16[4,2,128,128]{3,2,1,0:T(8,128)(2,1)S(1)}, bf16[4,2,128,128]{3,2,1,0:T(8,128)(2,1)S(1)}, u32[]{:S(2)}, u32[]{:S(2)}) collective-permute-start(bf16[4,2,128,128]{3,2,1,0:T(8,128)(2,1)S(1)} %slice.101), channel_id=1, source_target_pairs={{0,16},{16,0},{1,17},{17,1},{2,18},{18,2},{3,19},{19,3},{4,20},{20... | collective-permute-start | bytes 786440 | tf_op jit(solution)/shard_map/cond/branch_8_fun/ppermute | solution.py:250
  31.3 33.0 %collective-permute-start.57 = (bf16[4,2,128,128]{3,2,1,0:T(8,128)(2,1)S(1)}, bf16[4,2,128,128]{3,2,1,0:T(8,128)(2,1)S(1)}, u32[]{:S(2)}, u32[]{:S(2)}) collective-permute-start(bf16[4,2,128,128]{3,2,1,0:T(8,128)(2,1)S(1)} %slice.101), channel_id=1, source_target_pairs={{32,160},{64,192},{96,224},{128,256},{288,416},{320,448},{352,480}... | collective-permute-start | bytes 786440 | tf_op jit(solution)/shard_map/cond/branch_8_fun/ppermute | solution.py:242
  32.6 23.3 %copy-start.9 = (bf16[128,512]{1,0:T(8,128)(2,1)S(1)}, bf16[128,512]{1,0:T(8,128)(2,1)}, u32[]{:S(2)}) copy-start(bf16[128,512]{1,0:T(8,128)(2,1)} %get-tuple-element.275.residual) | copy-start | bytes 393220
  32.6 19.5 %collective-permute-start.59 = (bf16[1,2,128,128]{3,2,1,0:T(8,128)(2,1)S(1)}, bf16[1,2,128,128]{3,2,1,0:T(8,128)(2,1)S(1)}, u32[]{:S(2)}, u32[]{:S(2)}) collective-permute-start(bf16[1,2,128,128]{3,2,1,0:T(8,128)(2,1)S(1)} %slice.102), channel_id=1, source_target_pairs={{160,416},{192,448},{224,480},{256,0},{416,160},{448,192},{480,224... | collective-permute-start | bytes 196616 | tf_op jit(solution)/shard_map/cond/branch_8_fun/ppermute | solution.py:242
  40.4 11.7 %collective-permute-start.60 = (bf16[1,2,128,128]{3,2,1,0:T(8,128)(2,1)S(1)}, bf16[1,2,128,128]{3,2,1,0:T(8,128)(2,1)S(1)}, u32[]{:S(2)}, u32[]{:S(2)}) collective-permute-start(bf16[1,2,128,128]{3,2,1,0:T(8,128)(2,1)S(1)} %slice.102), channel_id=1, source_target_pairs={{160,288},{192,320},{224,352},{256,384},{416,32},{448,64},{480,96}... | collective-permute-start | bytes 196616 | tf_op jit(solution)/shard_map/cond/branch_8_fun/ppermute | solution.py:242
  52.1 3.9 %copy-start.18 = (f32[7,512]{1,0:T(8,128)S(1)}, f32[7,512]{1,0:T(8,128)}, u32[]{:S(2)}) copy-start(f32[7,512]{1,0:T(8,128)} %get-tuple-element.278.taps_ref) | copy-start | bytes 43012
  52.1 5.2 %collective-permute-start.61 = (bf16[1,2,128,128]{3,2,1,0:T(8,128)(2,1)S(1)}, bf16[1,2,128,128]{3,2,1,0:T(8,128)(2,1)S(1)}, u32[]{:S(2)}, u32[]{:S(2)}) collective-permute-start(bf16[1,2,128,128]{3,2,1,0:T(8,128)(2,1)S(1)} %add.26.refs_1_), channel_id=1, source_target_pairs={{0,16},{16,0},{1,17},{17,1},{2,18},{18,2},{3,19},{19,3},{4,20},{20... | collective-permute-start | bytes 196616 | tf_op jit(solution)/shard_map/cond/branch_8_fun/ppermute | solution.py:262
  64.2 5.0 %collective-permute-start.62 = (bf16[4,2,128,128]{3,2,1,0:T(8,128)(2,1)S(1)}, bf16[4,2,128,128]{3,2,1,0:T(8,128)(2,1)S(1)}, u32[]{:S(2)}, u32[]{:S(2)}) collective-permute-start(bf16[4,2,128,128]{3,2,1,0:T(8,128)(2,1)S(1)} %collective-permute-done.57.refs_0_), channel_id=1, source_target_pairs={{0,16},{16,0},{1,17},{17,1},{2,18},{18,2},{3,19},{19,3},{4,20},{20... | collective-permute-start | bytes 786440 | tf_op jit(solution)/shard_map/cond/branch_8_fun/ppermute | solution.py:265
  97.1 21.6 %all-to-all-start.19 = ((f32[32,1,128]{2,1,0:T(1,128)}), f32[32,1,128]{2,1,0:T(1,128)S(1)}, u32[]{:S(2)}, u32[]{:S(2)}) async-start(f32[32,1,128]{2,1,0:T(1,128)} %get-tuple-element.306), calls=%async_computation.19 | async-start | bytes 32768 | tf_op jit(solution)/shard_map/record_energy/all_to_all | solution.py:316
  108.6 10.1 %copy-start.29 = (s32[16]{0:T(128)S(1)}, s32[16]{0:T(128)}, u32[]{:S(2)}) copy-start(s32[16]{0:T(128)} %lengths.1) | copy-start | bytes 196

commit v2 on v1

--- a/solution.py
+++ b/solution.py
@@ -135,7 +135,7 @@
         sources = [before(refs[0], core if phase == 1 else 1 - core)]
         state, outs = refs[1:4], refs[4:]
 
-    @pl.loop(0, GROUP)
+    @pl.loop(0, GROUP, unroll=2 if phase else 1)
     def _(block):
         query_first = chip_position(cut, group, block, core, rows)
         query_pos = query_first + place
@@ -248,7 +248,6 @@
     before = along(key_value, 1, evens)
     last = received[GROUP - 1 :, 1:]
     other = lax.ppermute(key_value, "core", swap)
-    last, streams, other = lax.optimization_barrier((last, streams, other))
     edge = along(last, 2, odds) + along(last, 1, odds)
     base = pl.pallas_call(
         hyena_kernel,

time: 119 us -> 119 us (level); the launches traced: 119 us -> 118 us
  blocking collectives: 22.6 us -> 31.2 us
  waiting for transfers between devices: 30.7 us -> 23.3 us
  starting transfers between devices: 47.1 us -> 45.3 us
    all_to_all x1, blocking collectives: 9.43 us -> 18.1 us  [mixers(): heads = lax.all_to_all(out, 'z', 0, 0, axis_index_groups=groups, tiled=True)]
    ppermute x3, starting transfers between devices: 10.7 us -> 4.96 us  [along(): return lax.ppermute(value, 'z', pairs)]
    ppermute x3, waiting for transfers between devices: 13.9 us -> 8.44 us  [along(): return lax.ppermute(value, 'z', pairs)]
    all_to_all x1, starting transfers between devices: 9.78 us -> 14.5 us  [on_device(): sums = lax.all_to_all(sums, POSITIONS, 0, 0, tiled=True)]
    all_to_all x1, waiting for transfers between devices: 6.63 us -> 4.57 us  [mixers(): lax.all_to_all(packed, 'z', 0, 0, axis_index_groups=groups, tiled=True)]
    ppermute x1, starting transfers between devices: 2.13 us -> 3.92 us  [mixers(): lax.ppermute(streams[1:, rows - 16:], POSITIONS, [(i, i + 1) for i in ran...]
where the time goes in v2:
time: 119 us; the launch traced here: 118 us
  starting transfers between devices  45.3 us (38%)
  blocking collectives  31.2 us (26%)
  waiting for transfers between devices  23.3 us (20%)
  Pallas kernels  14.8 us (12%)
  between operations  1.33 us (1%)
    all_to_all x1, blocking collectives, mixers(): heads = lax.all_to_all(out, 'z', 0, 0, axis_index_groups=groups, tiled=True)  18.1 us
    all_to_all x1, starting transfers between devices, on_device(): sums = lax.all_to_all(sums, POSITIONS, 0, 0, tiled=True)  14.5 us
    all_to_all x1, starting transfers between devices, mixers(): lax.all_to_all(packed, 'z', 0, 0, axis_index_groups=groups, tiled=True)  13.5 us
    all_to_all x1, blocking collectives, on_device(): parts = lax.all_to_all(squares, 'mp', 0, 0, tiled=True)  13.2 us
    all_to_all x1, waiting for transfers between devices, on_device(): sums = lax.all_to_all(sums, POSITIONS, 0, 0, tiled=True)  10.1 us
    ppermute x3, waiting for transfers between devices, along(): return lax.ppermute(value, 'z', pairs)  8.44 us
    pallas_call x3, Pallas kernels, attend(): pl.pallas_call(functools.partial(attend_kernel, long_chip, phase), out_sh...  7.68 us
    ppermute x3, starting transfers between devices, along(): return lax.ppermute(value, 'z', pairs)  4.96 us
  transfers between devices with their start and end apart: 9, of which 4 were waited for; matrix products, arithmetic and copies ran while one was open for 0% of the time, Pallas kernels for 7%

profile of v2, /device:TPU:1, one launch (start us, length us, event | category | flops | bytes accessed | tf_op | source)
XLA Modules:
  0.0 118.0 jit_solution(5403182992814272822)
XLA Ops:
  0.6 0.0 copy-start.19
  0.6 0.0 copy-start
  0.7 0.6 copy-done.19
  1.3 1.8 %pack_heads.1 = (bf16[4,3,128,128]{3,2,1,0:T(8,128)(2,1)}, s32[2,1,128]{2,1,0:T(1,128)}, s32[1]{0:T(128)}) custom-call(s32[16]{0:T(128)S(1)} %copy-done.19, s32[16]{0:T(128)} %lengths.1, bf16[3,128,512]{2,1,0:T(8,128)(2,1)} %bitcast.13), custom_call_target="tpu_custom_call" | custom-call | tf_op jit(solution)/shard_map/pack_heads/pallas_call | solution.py:49
  3.8 0.0 copy-done
  3.8 71.9 %conditional.4 = (f32[128,512]{1,0:T(8,128)S(1)}, f32[4,128,128]{2,1,0:T(8,128)S(1)}) conditional(s32[]{:T(128)} %bitcast.1, (bf16[4,3,128,128]{3,2,1,0:T(8,128)(2,1)}, bf16[3,128,512]{2,1,0:T(8,128)(2,1)S(1)}, s32[16]{0:T(128)S(1)}, bf16[128,512]{1,0:T(8,128)(2,1)}, f32[7,512]{1,0:T(8,128)}) %tuple.139, ...), branch_computations={%region_0.0_spmd, %region_1.0_spmd, %region_2.0_spmd, %region_3.0_... | conditional | flops 4020163840 | bytes 12116380
  4.1 13.5 %all-to-all-start.12 = ((bf16[4,3,128,128]{3,2,1,0:T(8,128)(2,1)}), bf16[4,3,128,128]{3,2,1,0:T(8,128)(2,1)S(1)}, u32[]{:S(2)}, u32[]{:S(2)}) async-start(bf16[4,3,128,128]{3,2,1,0:T(8,128)(2,1)} %get-tuple-element.206), calls=%async_computation.12 | async-start | bytes 786432 | tf_op jit(solution)/shard_map/cond/branch_6_fun/all_to_all | solution.py:246
  17.5 3.9 %collective-permute-start.42 = (bf16[2,16,512]{2,1,0:T(8,128)(2,1)S(1)}, bf16[2,16,512]{2,1,0:T(8,128)(2,1)S(1)}, u32[]{:S(2)}, u32[]{:S(2)}) collective-permute-start(bf16[2,16,512]{2,1,0:T(8,128)(2,1)S(1)} %slice.75), channel_id=1, source_target_pairs={{0,16},{16,32},{32,48},{48,64},{64,80},{80,96},{96,112},{112,128},... | collective-permute-start | bytes 98312 | tf_op jit(solution)/shard_map/cond/branch_6_fun/ppermute | solution.py:245
  21.5 4.6 %all-to-all-done.12.q_ref = bf16[4,3,128,128]{3,2,1,0:T(8,128)(2,1)S(1)} async-done(((bf16[4,3,128,128]{3,2,1,0:T(8,128)(2,1)}), bf16[4,3,128,128]{3,2,1,0:T(8,128)(2,1)S(1)}, u32[]{:S(2)}, u32[]{:S(2)}) %all-to-all-start.12) | async-done | bytes 393248 | tf_op jit(solution)/shard_map/cond/branch_6_fun/all_to_all | solution.py:246
  26.1 0.2 collective-permute-done.42.rim
  26.3 0.0 copy-start.26
  26.3 3.6 %collective-permute-start.44 = (bf16[4,2,128,128]{3,2,1,0:T(8,128)(2,1)S(1)}, bf16[4,2,128,128]{3,2,1,0:T(8,128)(2,1)S(1)}, u32[]{:S(2)}, u32[]{:S(2)}) collective-permute-start(bf16[4,2,128,128]{3,2,1,0:T(8,128)(2,1)S(1)} %slice.97), channel_id=1, source_target_pairs={{0,16},{16,0},{1,17},{17,1},{2,18},{18,2},{3,19},{19,3},{4,20},{20... | collective-permute-start | bytes 786440 | tf_op jit(solution)/shard_map/cond/branch_6_fun/ppermute | solution.py:250
  29.9 2.9 %collective-permute-start.43 = (bf16[4,2,128,128]{3,2,1,0:T(8,128)(2,1)S(1)}, bf16[4,2,128,128]{3,2,1,0:T(8,128)(2,1)S(1)}, u32[]{:S(2)}, u32[]{:S(2)}) collective-permute-start(bf16[4,2,128,128]{3,2,1,0:T(8,128)(2,1)S(1)} %slice.97), channel_id=1, source_target_pairs={{224,352},{256,384},{288,416},{320,448},{480,96},{0,128},{32,160},... | collective-permute-start | bytes 786440 | tf_op jit(solution)/shard_map/cond/branch_6_fun/ppermute | solution.py:242
  32.8 0.0 copy-done.26
  32.8 0.0 copy-start.7
  32.8 0.8 collective-permute-start.45
  33.6 1.3 %collective-permute-start.46 = (bf16[1,2,128,128]{3,2,1,0:T(8,128)(2,1)S(1)}, bf16[1,2,128,128]{3,2,1,0:T(8,128)(2,1)S(1)}, u32[]{:S(2)}, u32[]{:S(2)}) collective-permute-start(bf16[1,2,128,128]{3,2,1,0:T(8,128)(2,1)S(1)} %slice.98), channel_id=1, source_target_pairs={{96,224},{128,256},{160,288},{192,320},{352,480},{384,0},{416,32},... | collective-permute-start | bytes 196616 | tf_op jit(solution)/shard_map/cond/branch_6_fun/ppermute | solution.py:242
  34.9 0.0 collective-permute-done.45
  34.9 8.4 %collective-permute-done.46 = bf16[1,2,128,128]{3,2,1,0:T(8,128)(2,1)S(1)} collective-permute-done((bf16[1,2,128,128]{3,2,1,0:T(8,128)(2,1)S(1)}, bf16[1,2,128,128]{3,2,1,0:T(8,128)(2,1)S(1)}, u32[]{:S(2)}, u32[]{:S(2)}) %collective-permute-start.46) | collective-permute-done | bytes 65568 | tf_op jit(solution)/shard_map/cond/branch_6_fun/ppermute | solution.py:242
  43.3 0.0 copy-start.16
  43.4 2.9 %collective-permute-start.47 = (bf16[1,2,128,128]{3,2,1,0:T(8,128)(2,1)S(1)}, bf16[1,2,128,128]{3,2,1,0:T(8,128)(2,1)S(1)}, u32[]{:S(2)}, u32[]{:S(2)}) collective-permute-start(bf16[1,2,128,128]{3,2,1,0:T(8,128)(2,1)S(1)} %add.24.refs_1_), channel_id=1, source_target_pairs={{0,16},{16,0},{1,17},{17,1},{2,18},{18,2},{3,19},{19,3},{4,20},{20... | collective-permute-start | bytes 196616 | tf_op jit(solution)/shard_map/cond/branch_6_fun/ppermute | solution.py:261
  46.3 0.0 copy-done.7
  46.3 0.0 copy-done.16
  46.3 1.3 %hyena.15 = f32[128,512]{1,0:T(8,128)S(1)} custom-call(s32[16]{0:T(128)S(1)} %get-tuple-element.209.starts, bf16[128,512]{1,0:T(8,128)(2,1)S(1)} %copy-done.7, bf16[3,128,512]{2,1,0:T(8,128)(2,1)S(1)} %get-tuple-element.207.streams, bf16[2,16,512]{2,1,0:T(8,128)(2,1)} %copy-done.26, f32[7,512]{1,0:T(8,128)S(1)} %copy-done.16), custom_call_target="tpu_custom_call" | custom-call | flops 10000000 | bytes 1048576 | tf_op jit(solution)/shard_map/cond/branch_6_fun/hyena/pallas_call | solution.py:252
  47.6 0.0 collective-permute-done.47.refs_2_
  47.6 0.0 collective-permute-done.44.refs_0_
  47.6 3.1 %attend0.15 = (f32[4,128,1]{2,1,0:T(8,128)S(1)}, f32[4,128,1]{2,1,0:T(8,128)S(1)}, f32[4,128,128]{2,1,0:T(8,128)S(1)}) custom-call(s32[16]{0:T(128)S(1)} %get-tuple-element.209.starts, bf16[4,3,128,128]{3,2,1,0:T(8,128)(2,1)S(1)} %all-to-all-done.12.q_ref, bf16[4,2,128,128]{3,2,1,0:T(8,128)(2,1)S(1)} %collective-permute-done.44.refs_0_, ...), custom_call_target="tpu_custom_call" | custom-call | flops 10000000 | bytes 1048576 | tf_op jit(solution)/shard_map/cond/branch_6_fun/attend0/pallas_call | solution.py:165
  50.7 0.0 collective-permute-done.43.refs_0_
  50.7 1.9 %collective-permute-start.48 = (bf16[4,2,128,128]{3,2,1,0:T(8,128)(2,1)S(1)}, bf16[4,2,128,128]{3,2,1,0:T(8,128)(2,1)S(1)}, u32[]{:S(2)}, u32[]{:S(2)}) collective-permute-start(bf16[4,2,128,128]{3,2,1,0:T(8,128)(2,1)S(1)} %collective-permute-done.43.refs_0_), channel_id=1, source_target_pairs={{0,16},{16,0},{1,17},{17,1},{2,18},{18,2},{3,19},{19,3},{4,20},{20... | collective-permute-start | bytes 786440 | tf_op jit(solution)/shard_map/cond/branch_6_fun/ppermute | solution.py:264
  52.7 2.3 %attend1.15 = (f32[4,128,1]{2,1,0:T(8,128)S(1)}, f32[4,128,1]{2,1,0:T(8,128)S(1)}, f32[4,128,128]{2,1,0:T(8,128)S(1)}) custom-call(s32[16]{0:T(128)S(1)} %get-tuple-element.209.starts, bf16[4,3,128,128]{3,2,1,0:T(8,128)(2,1)S(1)} %all-to-all-done.12.q_ref, bf16[4,2,128,128]{3,2,1,0:T(8,128)(2,1)S(1)} %collective-permute-done.43.refs_0_, ...), custom_call_target="tpu_custom_call" | custom-call | flops 2000000000 | bytes 1048576 | tf_op jit(solution)/shard_map/cond/branch_6_fun/attend1/pallas_call | solution.py:165
  54.9 0.0 collective-permute-done.48.refs_0_
  54.9 2.4 %attend2.15 = f32[4,128,128]{2,1,0:T(8,128)S(1)} custom-call(s32[16]{0:T(128)S(1)} %get-tuple-element.209.starts, bf16[4,3,128,128]{3,2,1,0:T(8,128)(2,1)S(1)} %all-to-all-done.12.q_ref, bf16[4,2,128,128]{3,2,1,0:T(8,128)(2,1)S(1)} %collective-permute-done.48.refs_0_, f32[4,128,1]{2,1,0:T(8,128)S(1)} %get-tuple-element.221.refs_1_, ...), custom_call_target="tpu_custom_call" | custom-call | flops 2000000000 | bytes 1048576 | tf_op jit(solution)/shard_map/cond/branch_6_fun/attend2/pallas_call | solution.py:165
  57.3 18.1 %all_to_all.88 = f16[4,128,128]{2,1,0:T(8,128)(2,1)S(1)} all-to-all(f16[4,128,128]{2,1,0:T(8,128)(2,1)S(1)} %convert_element_type.70), channel_id=1, replica_groups={{96,128,160,192},{224,256,288,320},{352,384,416,448},{480,0,32,64},{97,..., dimensions={0} | all-to-all | bytes 262144 | tf_op jit(solution)/shard_map/cond/branch_6_fun/all_to_all | solution.py:268
  75.7 0.7 stream.1
  76.5 13.2 %all_to_all.91.parts = f32[16,1,128]{2,1,0:T(1,128)} all-to-all(f32[16,1,128]{2,1,0:T(1,128)} %get-tuple-element.277), channel_id=1, replica_groups=mesh['z'=16,'core'=2,'mp'=16] {'mp'}, dimensions={0} | all-to-all | bytes 16384 | tf_op jit(solution)/shard_map/mean_square/all_to_all | solution.py:305
  89.6 1.4 %records.1 = (f32[128,128]{1,0:T(8,128)}, f32[32,1,128]{2,1,0:T(1,128)}) custom-call(s32[2,1,128]{2,1,0:T(1,128)} %get-tuple-element.276.lines, f32[16,1,128]{2,1,0:T(1,128)} %all_to_all.91.parts), custom_call_target="tpu_custom_call" | custom-call | tf_op jit(solution)/shard_map/record_energy/records/pallas_call | solution.py:307
  91.1 14.5 %all-to-all-start.19 = ((f32[32,1,128]{2,1,0:T(1,128)}), f32[32,1,128]{2,1,0:T(1,128)S(1)}, u32[]{:S(2)}, u32[]{:S(2)}) async-start(f32[32,1,128]{2,1,0:T(1,128)} %get-tuple-element.279), calls=%async_computation.19 | async-start | bytes 32768 | tf_op jit(solution)/shard_map/record_energy/all_to_all | solution.py:315
  105.6 1.7 %scale.1 = f32[128,512]{1,0:T(8,128)} custom-call(f32[128,512]{1,0:T(8,128)} %get-tuple-element.275.stream, f32[128,128]{1,0:T(8,128)} %get-tuple-element.278.mean, f32[1,512]{1,0:T(1,128)} %bitcast.14), custom_call_target="tpu_custom_call" | custom-call | flops 1000000000 | bytes 1048576 | tf_op jit(solution)/shard_map/scale/pallas_call | solution.py:317
  107.3 0.0 copy-start.29
  107.3 10.1 %all-to-all-done.19 = f32[32,1,128]{2,1,0:T(1,128)S(1)} async-done(((f32[32,1,128]{2,1,0:T(1,128)}), f32[32,1,128]{2,1,0:T(1,128)S(1)}, u32[]{:S(2)}, u32[]{:S(2)}) %all-to-all-start.19) | async-done | bytes 16416 | tf_op jit(solution)/shard_map/record_energy/all_to_all | solution.py:315
  117.4 0.1 reduce_sum.9
  117.5 0.0 copy-done.29
  117.5 0.5 convert_divide_fusion
  (6 shorter events, 0.1 us)
Async XLA Ops:
  0.6 0.7 copy-start.19
  0.6 3.1 %copy-start = (bf16[128,3,512]{2,0,1:T(8,128)(2,1)S(1)}, bf16[128,3,512]{2,0,1:T(8,128)(2,1)}, u32[]{:S(2)}) copy-start(bf16[128,3,512]{2,0,1:T(8,128)(2,1)} %param.18) | copy-start | bytes 1179652
  4.1 22.0 %all-to-all-start.12 = ((bf16[4,3,128,128]{3,2,1,0:T(8,128)(2,1)}), bf16[4,3,128,128]{3,2,1,0:T(8,128)(2,1)S(1)}, u32[]{:S(2)}, u32[]{:S(2)}) async-start(bf16[4,3,128,128]{3,2,1,0:T(8,128)(2,1)} %get-tuple-element.206), calls=%async_computation.12 | async-start | bytes 786432 | tf_op jit(solution)/shard_map/cond/branch_6_fun/all_to_all | solution.py:246
  17.5 8.8 %collective-permute-start.42 = (bf16[2,16,512]{2,1,0:T(8,128)(2,1)S(1)}, bf16[2,16,512]{2,1,0:T(8,128)(2,1)S(1)}, u32[]{:S(2)}, u32[]{:S(2)}) collective-permute-start(bf16[2,16,512]{2,1,0:T(8,128)(2,1)S(1)} %slice.75), channel_id=1, source_target_pairs={{0,16},{16,32},{32,48},{48,64},{64,80},{80,96},{96,112},{112,128},... | collective-permute-start | bytes 98312 | tf_op jit(solution)/shard_map/cond/branch_6_fun/ppermute | solution.py:245
  26.3 6.5 %copy-start.26 = (bf16[2,16,512]{2,1,0:T(8,128)(2,1)}, bf16[2,16,512]{2,1,0:T(8,128)(2,1)S(1)}, u32[]{:S(2)}) copy-start(bf16[2,16,512]{2,1,0:T(8,128)(2,1)S(1)} %collective-permute-done.42.rim) | copy-start | bytes 98308
  26.3 21.3 %collective-permute-start.44 = (bf16[4,2,128,128]{3,2,1,0:T(8,128)(2,1)S(1)}, bf16[4,2,128,128]{3,2,1,0:T(8,128)(2,1)S(1)}, u32[]{:S(2)}, u32[]{:S(2)}) collective-permute-start(bf16[4,2,128,128]{3,2,1,0:T(8,128)(2,1)S(1)} %slice.97), channel_id=1, source_target_pairs={{0,16},{16,0},{1,17},{17,1},{2,18},{18,2},{3,19},{19,3},{4,20},{20... | collective-permute-start | bytes 786440 | tf_op jit(solution)/shard_map/cond/branch_6_fun/ppermute | solution.py:250
  29.9 20.8 %collective-permute-start.43 = (bf16[4,2,128,128]{3,2,1,0:T(8,128)(2,1)S(1)}, bf16[4,2,128,128]{3,2,1,0:T(8,128)(2,1)S(1)}, u32[]{:S(2)}, u32[]{:S(2)}) collective-permute-start(bf16[4,2,128,128]{3,2,1,0:T(8,128)(2,1)S(1)} %slice.97), channel_id=1, source_target_pairs={{224,352},{256,384},{288,416},{320,448},{480,96},{0,128},{32,160},... | collective-permute-start | bytes 786440 | tf_op jit(solution)/shard_map/cond/branch_6_fun/ppermute | solution.py:242
  32.8 13.5 %copy-start.7 = (bf16[128,512]{1,0:T(8,128)(2,1)S(1)}, bf16[128,512]{1,0:T(8,128)(2,1)}, u32[]{:S(2)}) copy-start(bf16[128,512]{1,0:T(8,128)(2,1)} %get-tuple-element.213.residual) | copy-start | bytes 393220
  32.8 2.1 %collective-permute-start.45 = (bf16[1,2,128,128]{3,2,1,0:T(8,128)(2,1)S(1)}, bf16[1,2,128,128]{3,2,1,0:T(8,128)(2,1)S(1)}, u32[]{:S(2)}, u32[]{:S(2)}) collective-permute-start(bf16[1,2,128,128]{3,2,1,0:T(8,128)(2,1)S(1)} %slice.98), channel_id=1, source_target_pairs={{96,352},{128,384},{160,416},{192,448},{352,96},{384,128},{416,160... | collective-permute-start | bytes 196616 | tf_op jit(solution)/shard_map/cond/branch_6_fun/ppermute | solution.py:242
  33.6 9.8 %collective-permute-start.46 = (bf16[1,2,128,128]{3,2,1,0:T(8,128)(2,1)S(1)}, bf16[1,2,128,128]{3,2,1,0:T(8,128)(2,1)S(1)}, u32[]{:S(2)}, u32[]{:S(2)}) collective-permute-start(bf16[1,2,128,128]{3,2,1,0:T(8,128)(2,1)S(1)} %slice.98), channel_id=1, source_target_pairs={{96,224},{128,256},{160,288},{192,320},{352,480},{384,0},{416,32},... | collective-permute-start | bytes 196616 | tf_op jit(solution)/shard_map/cond/branch_6_fun/ppermute | solution.py:242
  43.3 2.9 %copy-start.16 = (f32[7,512]{1,0:T(8,128)S(1)}, f32[7,512]{1,0:T(8,128)}, u32[]{:S(2)}) copy-start(f32[7,512]{1,0:T(8,128)} %get-tuple-element.215.taps_ref) | copy-start | bytes 43012
  43.4 4.3 %collective-permute-start.47 = (bf16[1,2,128,128]{3,2,1,0:T(8,128)(2,1)S(1)}, bf16[1,2,128,128]{3,2,1,0:T(8,128)(2,1)S(1)}, u32[]{:S(2)}, u32[]{:S(2)}) collective-permute-start(bf16[1,2,128,128]{3,2,1,0:T(8,128)(2,1)S(1)} %add.24.refs_1_), channel_id=1, source_target_pairs={{0,16},{16,0},{1,17},{17,1},{2,18},{18,2},{3,19},{19,3},{4,20},{20... | collective-permute-start | bytes 196616 | tf_op jit(solution)/shard_map/cond/branch_6_fun/ppermute | solution.py:261
  50.7 4.2 %collective-permute-start.48 = (bf16[4,2,128,128]{3,2,1,0:T(8,128)(2,1)S(1)}, bf16[4,2,128,128]{3,2,1,0:T(8,128)(2,1)S(1)}, u32[]{:S(2)}, u32[]{:S(2)}) collective-permute-start(bf16[4,2,128,128]{3,2,1,0:T(8,128)(2,1)S(1)} %collective-permute-done.43.refs_0_), channel_id=1, source_target_pairs={{0,16},{16,0},{1,17},{17,1},{2,18},{18,2},{3,19},{19,3},{4,20},{20... | collective-permute-start | bytes 786440 | tf_op jit(solution)/shard_map/cond/branch_6_fun/ppermute | solution.py:264
  91.1 26.3 %all-to-all-start.19 = ((f32[32,1,128]{2,1,0:T(1,128)}), f32[32,1,128]{2,1,0:T(1,128)S(1)}, u32[]{:S(2)}, u32[]{:S(2)}) async-start(f32[32,1,128]{2,1,0:T(1,128)} %get-tuple-element.279), calls=%async_computation.19 | async-start | bytes 32768 | tf_op jit(solution)/shard_map/record_energy/all_to_all | solution.py:315
  107.3 10.1 %copy-start.29 = (s32[16]{0:T(128)S(1)}, s32[16]{0:T(128)}, u32[]{:S(2)}) copy-start(s32[16]{0:T(128)} %lengths.1) | copy-start | bytes 196

commit v3 on v1

--- a/solution.py
+++ b/solution.py
@@ -313,7 +313,7 @@
             ),
             name="records",
         )(lines, parts)
-        sums = lax.all_to_all(sums, POSITIONS, 0, 0, tiled=True)
+        sums = lax.all_to_all(sums, ("core", "z"), 0, 0, tiled=True)
         record_energy = jnp.sum(sums, axis=(0, 1))[:records] / record_lengths.astype(jnp.float32)
     mixed = pl.pallas_call(
         scale_kernel,

time: 119 us -> 120 us (level)
  waiting for transfers between devices: 30.7 us -> 22 us
  blocking collectives: 22.6 us -> 31.2 us
    all_to_all x1, blocking collectives: 9.43 us -> 18.1 us  [mixers(): heads = lax.all_to_all(out, 'z', 0, 0, axis_index_groups=groups, tiled=True)]
    ppermute x3, waiting for transfers between devices: 13.9 us -> 6.93 us  [along(): return lax.ppermute(value, 'z', pairs)]
    all_to_all x1, waiting for transfers between devices: 6.63 us -> 4.57 us  [mixers(): lax.all_to_all(packed, 'z', 0, 0, axis_index_groups=groups, tiled=True)]
    ppermute x1, starting transfers between devices: 2.13 us -> 3.92 us  [mixers(): lax.ppermute(streams[1:, rows - 16:], POSITIONS, [(i, i + 1) for i in ran...]
  transfers between devices with their start and end apart: 9 -> 9, of which waited for: 4 -> 5; matrix products, arithmetic and copies ran while one was open for 0% -> 0% of each run, Pallas kernels for 7% -> 7%
where the time goes in v3:
time: 120 us
  starting transfers between devices  47.6 us (40%)
  blocking collectives  31.2 us (26%)
  waiting for transfers between devices  22 us (18%)
  Pallas kernels  15.5 us (13%)
  between operations  1.33 us (1%)
    all_to_all x1, blocking collectives, mixers(): heads = lax.all_to_all(out, 'z', 0, 0, axis_index_groups=groups, tiled=True)  18.1 us
    all_to_all x1, starting transfers between devices, mixers(): lax.all_to_all(packed, 'z', 0, 0, axis_index_groups=groups, tiled=True)  13.5 us
    all_to_all x1, blocking collectives, on_device(): parts = lax.all_to_all(squares, 'mp', 0, 0, tiled=True)  13.2 us
    ppermute x3, starting transfers between devices, along(): return lax.ppermute(value, 'z', pairs)  10.7 us
    all_to_all x1, waiting for transfers between devices, on_device(): sums = lax.all_to_all(sums, ('core', 'z'), 0, 0, tiled=True)  10.2 us
    all_to_all x1, starting transfers between devices, on_device(): sums = lax.all_to_all(sums, ('core', 'z'), 0, 0, tiled=True)  10.1 us
    pallas_call x3, Pallas kernels, attend(): pl.pallas_call(functools.partial(attend_kernel, long_chip, phase), out_sh...  8.41 us
    ppermute x3, waiting for transfers between devices, along(): return lax.ppermute(value, 'z', pairs)  6.93 us
  transfers between devices with their start and end apart: 9, of which 5 were waited for; matrix products, arithmetic and copies ran while one was open for 0% of the time, Pallas kernels for 7%

profile of v3, /device:TPU:1, one launch (start us, length us, event | category | flops | bytes accessed | tf_op | source)
XLA Modules:
  0.0 119.6 jit_solution(1788405894449114943)
XLA Ops:
  0.6 0.0 copy-start.19
  0.6 0.0 copy-start
  0.7 0.6 copy-done.19
  1.3 1.8 %pack_heads.1 = (bf16[4,3,128,128]{3,2,1,0:T(8,128)(2,1)}, s32[2,1,128]{2,1,0:T(1,128)}, s32[1]{0:T(128)}) custom-call(s32[16]{0:T(128)S(1)} %copy-done.19, s32[16]{0:T(128)} %lengths.1, bf16[3,128,512]{2,1,0:T(8,128)(2,1)} %bitcast.13), custom_call_target="tpu_custom_call" | custom-call | tf_op jit(solution)/shard_map/pack_heads/pallas_call | solution.py:49
  3.8 0.0 copy-done
  3.8 77.7 %conditional.4 = (f32[128,512]{1,0:T(8,128)S(1)}, f32[4,128,128]{2,1,0:T(8,128)S(1)}) conditional(s32[]{:T(128)} %bitcast.1, (bf16[4,3,128,128]{3,2,1,0:T(8,128)(2,1)}, bf16[3,128,512]{2,1,0:T(8,128)(2,1)S(1)}, s32[16]{0:T(128)S(1)}, bf16[128,512]{1,0:T(8,128)(2,1)}, f32[7,512]{1,0:T(8,128)}) %tuple.148, ...), branch_computations={%region_0.0_spmd, %region_1.0_spmd, %region_2.0_spmd, %region_3.0_... | conditional | flops 4020163840 | bytes 12116380
  3.8 13.5 %all-to-all-start.4 = ((bf16[4,3,128,128]{3,2,1,0:T(8,128)(2,1)}), bf16[4,3,128,128]{3,2,1,0:T(8,128)(2,1)S(1)}, u32[]{:S(2)}, u32[]{:S(2)}) async-start(bf16[4,3,128,128]{3,2,1,0:T(8,128)(2,1)} %get-tuple-element.140), calls=%async_computation.4 | async-start | bytes 786432 | tf_op jit(solution)/shard_map/cond/branch_2_fun/all_to_all | solution.py:246
  17.3 3.9 %collective-permute-start.14 = (bf16[2,16,512]{2,1,0:T(8,128)(2,1)S(1)}, bf16[2,16,512]{2,1,0:T(8,128)(2,1)S(1)}, u32[]{:S(2)}, u32[]{:S(2)}) collective-permute-start(bf16[2,16,512]{2,1,0:T(8,128)(2,1)S(1)} %slice.63), channel_id=1, source_target_pairs={{0,16},{16,32},{32,48},{48,64},{64,80},{80,96},{96,112},{112,128},... | collective-permute-start | bytes 98312 | tf_op jit(solution)/shard_map/cond/branch_2_fun/ppermute | solution.py:245
  21.2 4.6 %all-to-all-done.4.q_ref = bf16[4,3,128,128]{3,2,1,0:T(8,128)(2,1)S(1)} async-done(((bf16[4,3,128,128]{3,2,1,0:T(8,128)(2,1)}), bf16[4,3,128,128]{3,2,1,0:T(8,128)(2,1)S(1)}, u32[]{:S(2)}, u32[]{:S(2)}) %all-to-all-start.4) | async-done | bytes 393248 | tf_op jit(solution)/shard_map/cond/branch_2_fun/all_to_all | solution.py:246
  25.8 0.2 collective-permute-done.14.rim
  26.1 0.0 copy-start.22
  26.1 3.6 %collective-permute-start.16 = (bf16[4,2,128,128]{3,2,1,0:T(8,128)(2,1)S(1)}, bf16[4,2,128,128]{3,2,1,0:T(8,128)(2,1)S(1)}, u32[]{:S(2)}, u32[]{:S(2)}) collective-permute-start(bf16[4,2,128,128]{3,2,1,0:T(8,128)(2,1)S(1)} %slice.89), channel_id=1, source_target_pairs={{0,16},{16,0},{1,17},{17,1},{2,18},{18,2},{3,19},{19,3},{4,20},{20... | collective-permute-start | bytes 786440 | tf_op jit(solution)/shard_map/cond/branch_2_fun/ppermute | solution.py:250
  29.6 1.3 %collective-permute-start.15 = (bf16[4,2,128,128]{3,2,1,0:T(8,128)(2,1)S(1)}, bf16[4,2,128,128]{3,2,1,0:T(8,128)(2,1)S(1)}, u32[]{:S(2)}, u32[]{:S(2)}) collective-permute-start(bf16[4,2,128,128]{3,2,1,0:T(8,128)(2,1)S(1)} %slice.89), channel_id=1, source_target_pairs={{96,224},{128,256},{160,288},{192,320},{352,480},{384,0},{416,32},... | collective-permute-start | bytes 786440 | tf_op jit(solution)/shard_map/cond/branch_2_fun/ppermute | solution.py:242
  31.0 0.0 copy-done.22
  31.0 0.0 copy-start.3
  31.0 0.0 collective-permute-done.16.refs_0_
  31.0 7.8 %collective-permute-start.17 = (bf16[1,2,128,128]{3,2,1,0:T(8,128)(2,1)S(1)}, bf16[1,2,128,128]{3,2,1,0:T(8,128)(2,1)S(1)}, u32[]{:S(2)}, u32[]{:S(2)}) collective-permute-start(bf16[1,2,128,128]{3,2,1,0:T(8,128)(2,1)S(1)} %slice.90), channel_id=1, source_target_pairs={{224,480},{256,0},{288,32},{320,64},{480,224},{0,256},{32,288},{64... | collective-permute-start | bytes 196616 | tf_op jit(solution)/shard_map/cond/branch_2_fun/ppermute | solution.py:242
  38.8 1.6 %collective-permute-start.18 = (bf16[1,2,128,128]{3,2,1,0:T(8,128)(2,1)S(1)}, bf16[1,2,128,128]{3,2,1,0:T(8,128)(2,1)S(1)}, u32[]{:S(2)}, u32[]{:S(2)}) collective-permute-start(bf16[1,2,128,128]{3,2,1,0:T(8,128)(2,1)S(1)} %slice.90), channel_id=1, source_target_pairs={{224,352},{256,384},{288,416},{320,448},{480,96},{0,128},{32,160},... | collective-permute-start | bytes 196616 | tf_op jit(solution)/shard_map/cond/branch_2_fun/ppermute | solution.py:242
  40.4 5.2 %collective-permute-done.17 = bf16[1,2,128,128]{3,2,1,0:T(8,128)(2,1)S(1)} collective-permute-done((bf16[1,2,128,128]{3,2,1,0:T(8,128)(2,1)S(1)}, bf16[1,2,128,128]{3,2,1,0:T(8,128)(2,1)S(1)}, u32[]{:S(2)}, u32[]{:S(2)}) %collective-permute-start.17) | collective-permute-done | bytes 65568 | tf_op jit(solution)/shard_map/cond/branch_2_fun/ppermute | solution.py:242
  45.6 0.0 collective-permute-done.18
  45.6 0.0 copy-start.12
  45.7 3.0 %collective-permute-start.19 = (bf16[1,2,128,128]{3,2,1,0:T(8,128)(2,1)S(1)}, bf16[1,2,128,128]{3,2,1,0:T(8,128)(2,1)S(1)}, u32[]{:S(2)}, u32[]{:S(2)}) collective-permute-start(bf16[1,2,128,128]{3,2,1,0:T(8,128)(2,1)S(1)} %add.20.refs_1_), channel_id=1, source_target_pairs={{0,16},{16,0},{1,17},{17,1},{2,18},{18,2},{3,19},{19,3},{4,20},{20... | collective-permute-start | bytes 196616 | tf_op jit(solution)/shard_map/cond/branch_2_fun/ppermute | solution.py:262
  48.6 0.0 copy-done.3
  48.7 0.0 copy-done.12
  48.7 1.3 %hyena.11 = f32[128,512]{1,0:T(8,128)S(1)} custom-call(s32[16]{0:T(128)S(1)} %get-tuple-element.143.starts, bf16[128,512]{1,0:T(8,128)(2,1)S(1)} %copy-done.3, bf16[3,128,512]{2,1,0:T(8,128)(2,1)S(1)} %get-tuple-element.150.streams, bf16[2,16,512]{2,1,0:T(8,128)(2,1)} %copy-done.22, f32[7,512]{1,0:T(8,128)S(1)} %copy-done.12), custom_call_target="tpu_custom_call" | custom-call | flops 10000000 | bytes 1048576 | tf_op jit(solution)/shard_map/cond/branch_2_fun/hyena/pallas_call | solution.py:253
  50.0 0.0 collective-permute-done.19.refs_2_
  50.0 3.1 %attend0.11 = (f32[4,128,1]{2,1,0:T(8,128)S(1)}, f32[4,128,1]{2,1,0:T(8,128)S(1)}, f32[4,128,128]{2,1,0:T(8,128)S(1)}) custom-call(s32[16]{0:T(128)S(1)} %get-tuple-element.143.starts, bf16[4,3,128,128]{3,2,1,0:T(8,128)(2,1)S(1)} %all-to-all-done.4.q_ref, bf16[4,2,128,128]{3,2,1,0:T(8,128)(2,1)S(1)} %collective-permute-done.16.refs_0_, ...), custom_call_target="tpu_custom_call" | custom-call | flops 10000000 | bytes 1048576 | tf_op jit(solution)/shard_map/cond/branch_2_fun/attend0/pallas_call | solution.py:165
  53.1 1.7 %collective-permute-done.15.refs_0_ = bf16[4,2,128,128]{3,2,1,0:T(8,128)(2,1)S(1)} collective-permute-done((bf16[4,2,128,128]{3,2,1,0:T(8,128)(2,1)S(1)}, bf16[4,2,128,128]{3,2,1,0:T(8,128)(2,1)S(1)}, u32[]{:S(2)}, u32[]{:S(2)}) %collective-permute-start.15) | collective-permute-done | bytes 262176 | tf_op jit(solution)/shard_map/cond/branch_2_fun/ppermute | solution.py:242
  54.8 2.8 %collective-permute-start.20 = (bf16[4,2,128,128]{3,2,1,0:T(8,128)(2,1)S(1)}, bf16[4,2,128,128]{3,2,1,0:T(8,128)(2,1)S(1)}, u32[]{:S(2)}, u32[]{:S(2)}) collective-permute-start(bf16[4,2,128,128]{3,2,1,0:T(8,128)(2,1)S(1)} %collective-permute-done.15.refs_0_), channel_id=1, source_target_pairs={{0,16},{16,0},{1,17},{17,1},{2,18},{18,2},{3,19},{19,3},{4,20},{20... | collective-permute-start | bytes 786440 | tf_op jit(solution)/shard_map/cond/branch_2_fun/ppermute | solution.py:265
  57.6 2.6 %attend1.11 = (f32[4,128,1]{2,1,0:T(8,128)S(1)}, f32[4,128,1]{2,1,0:T(8,128)S(1)}, f32[4,128,128]{2,1,0:T(8,128)S(1)}) custom-call(s32[16]{0:T(128)S(1)} %get-tuple-element.143.starts, bf16[4,3,128,128]{3,2,1,0:T(8,128)(2,1)S(1)} %all-to-all-done.4.q_ref, bf16[4,2,128,128]{3,2,1,0:T(8,128)(2,1)S(1)} %collective-permute-done.15.refs_0_, ...), custom_call_target="tpu_custom_call" | custom-call | flops 2000000000 | bytes 1048576 | tf_op jit(solution)/shard_map/cond/branch_2_fun/attend1/pallas_call | solution.py:165
  60.2 0.0 collective-permute-done.20.refs_0_
  60.2 2.7 %attend2.11 = f32[4,128,128]{2,1,0:T(8,128)S(1)} custom-call(s32[16]{0:T(128)S(1)} %get-tuple-element.143.starts, bf16[4,3,128,128]{3,2,1,0:T(8,128)(2,1)S(1)} %all-to-all-done.4.q_ref, bf16[4,2,128,128]{3,2,1,0:T(8,128)(2,1)S(1)} %collective-permute-done.20.refs_0_, f32[4,128,1]{2,1,0:T(8,128)S(1)} %get-tuple-element.158.refs_1_, ...), custom_call_target="tpu_custom_call" | custom-call | flops 2000000000 | bytes 1048576 | tf_op jit(solution)/shard_map/cond/branch_2_fun/attend2/pallas_call | solution.py:165
  63.0 18.1 %all_to_all.84 = f16[4,128,128]{2,1,0:T(8,128)(2,1)S(1)} all-to-all(f16[4,128,128]{2,1,0:T(8,128)(2,1)S(1)} %convert_element_type.62), channel_id=1, replica_groups={{96,128,160,192},{224,256,288,320},{352,384,416,448},{480,0,32,64},{97,..., dimensions={0} | all-to-all | bytes 262144 | tf_op jit(solution)/shard_map/cond/branch_2_fun/all_to_all | solution.py:269
  81.5 0.7 stream.1
  82.3 13.2 %all_to_all.91.parts = f32[16,1,128]{2,1,0:T(1,128)} all-to-all(f32[16,1,128]{2,1,0:T(1,128)} %get-tuple-element.304), channel_id=1, replica_groups=mesh['z'=16,'core'=2,'mp'=16] {'mp'}, dimensions={0} | all-to-all | bytes 16384 | tf_op jit(solution)/shard_map/mean_square/all_to_all | solution.py:306
  95.5 1.4 %records.1 = (f32[128,128]{1,0:T(8,128)}, f32[32,1,128]{2,1,0:T(1,128)}) custom-call(s32[2,1,128]{2,1,0:T(1,128)} %get-tuple-element.303.lines, f32[16,1,128]{2,1,0:T(1,128)} %all_to_all.91.parts), custom_call_target="tpu_custom_call" | custom-call | tf_op jit(solution)/shard_map/record_energy/records/pallas_call | solution.py:308
  96.9 10.1 %all-to-all-start.19 = ((f32[32,1,128]{2,1,0:T(1,128)}), f32[32,1,128]{2,1,0:T(1,128)S(1)}, u32[]{:S(2)}, u32[]{:S(2)}) async-start(f32[32,1,128]{2,1,0:T(1,128)} %get-tuple-element.306), calls=%async_computation.19 | async-start | bytes 32768 | tf_op jit(solution)/shard_map/record_energy/all_to_all | solution.py:316
  107.1 1.7 %scale.1 = f32[128,512]{1,0:T(8,128)} custom-call(f32[128,512]{1,0:T(8,128)} %get-tuple-element.302.stream, f32[128,128]{1,0:T(8,128)} %get-tuple-element.305.mean, f32[1,512]{1,0:T(1,128)} %bitcast.14), custom_call_target="tpu_custom_call" | custom-call | flops 1000000000 | bytes 1048576 | tf_op jit(solution)/shard_map/scale/pallas_call | solution.py:318
  108.8 0.0 copy-start.29
  108.8 10.2 %all-to-all-done.19 = f32[32,1,128]{2,1,0:T(1,128)S(1)} async-done(((f32[32,1,128]{2,1,0:T(1,128)}), f32[32,1,128]{2,1,0:T(1,128)S(1)}, u32[]{:S(2)}, u32[]{:S(2)}) %all-to-all-start.19) | async-done | bytes 16416 | tf_op jit(solution)/shard_map/record_energy/all_to_all | solution.py:316
  119.0 0.1 reduce_sum.9
  119.1 0.0 copy-done.29
  119.1 0.5 convert_divide_fusion
  (6 shorter events, 0.1 us)
Async XLA Ops:
  0.6 0.7 copy-start.19
  0.6 3.1 %copy-start = (bf16[128,3,512]{2,0,1:T(8,128)(2,1)S(1)}, bf16[128,3,512]{2,0,1:T(8,128)(2,1)}, u32[]{:S(2)}) copy-start(bf16[128,3,512]{2,0,1:T(8,128)(2,1)} %param.18) | copy-start | bytes 1179652
  3.8 22.0 %all-to-all-start.4 = ((bf16[4,3,128,128]{3,2,1,0:T(8,128)(2,1)}), bf16[4,3,128,128]{3,2,1,0:T(8,128)(2,1)S(1)}, u32[]{:S(2)}, u32[]{:S(2)}) async-start(bf16[4,3,128,128]{3,2,1,0:T(8,128)(2,1)} %get-tuple-element.140), calls=%async_computation.4 | async-start | bytes 786432 | tf_op jit(solution)/shard_map/cond/branch_2_fun/all_to_all | solution.py:246
  17.3 8.8 %collective-permute-start.14 = (bf16[2,16,512]{2,1,0:T(8,128)(2,1)S(1)}, bf16[2,16,512]{2,1,0:T(8,128)(2,1)S(1)}, u32[]{:S(2)}, u32[]{:S(2)}) collective-permute-start(bf16[2,16,512]{2,1,0:T(8,128)(2,1)S(1)} %slice.63), channel_id=1, source_target_pairs={{0,16},{16,32},{32,48},{48,64},{64,80},{80,96},{96,112},{112,128},... | collective-permute-start | bytes 98312 | tf_op jit(solution)/shard_map/cond/branch_2_fun/ppermute | solution.py:245
  26.1 4.9 %copy-start.22 = (bf16[2,16,512]{2,1,0:T(8,128)(2,1)}, bf16[2,16,512]{2,1,0:T(8,128)(2,1)S(1)}, u32[]{:S(2)}) copy-start(bf16[2,16,512]{2,1,0:T(8,128)(2,1)S(1)} %collective-permute-done.14.rim) | copy-start | bytes 98308
  26.1 4.9 %collective-permute-start.16 = (bf16[4,2,128,128]{3,2,1,0:T(8,128)(2,1)S(1)}, bf16[4,2,128,128]{3,2,1,0:T(8,128)(2,1)S(1)}, u32[]{:S(2)}, u32[]{:S(2)}) collective-permute-start(bf16[4,2,128,128]{3,2,1,0:T(8,128)(2,1)S(1)} %slice.89), channel_id=1, source_target_pairs={{0,16},{16,0},{1,17},{17,1},{2,18},{18,2},{3,19},{19,3},{4,20},{20... | collective-permute-start | bytes 786440 | tf_op jit(solution)/shard_map/cond/branch_2_fun/ppermute | solution.py:250
  29.6 25.1 %collective-permute-start.15 = (bf16[4,2,128,128]{3,2,1,0:T(8,128)(2,1)S(1)}, bf16[4,2,128,128]{3,2,1,0:T(8,128)(2,1)S(1)}, u32[]{:S(2)}, u32[]{:S(2)}) collective-permute-start(bf16[4,2,128,128]{3,2,1,0:T(8,128)(2,1)S(1)} %slice.89), channel_id=1, source_target_pairs={{96,224},{128,256},{160,288},{192,320},{352,480},{384,0},{416,32},... | collective-permute-start | bytes 786440 | tf_op jit(solution)/shard_map/cond/branch_2_fun/ppermute | solution.py:242
  31.0 17.7 %copy-start.3 = (bf16[128,512]{1,0:T(8,128)(2,1)S(1)}, bf16[128,512]{1,0:T(8,128)(2,1)}, u32[]{:S(2)}) copy-start(bf16[128,512]{1,0:T(8,128)(2,1)} %get-tuple-element.149.residual) | copy-start | bytes 393220
  31.0 14.6 %collective-permute-start.17 = (bf16[1,2,128,128]{3,2,1,0:T(8,128)(2,1)S(1)}, bf16[1,2,128,128]{3,2,1,0:T(8,128)(2,1)S(1)}, u32[]{:S(2)}, u32[]{:S(2)}) collective-permute-start(bf16[1,2,128,128]{3,2,1,0:T(8,128)(2,1)S(1)} %slice.90), channel_id=1, source_target_pairs={{224,480},{256,0},{288,32},{320,64},{480,224},{0,256},{32,288},{64... | collective-permute-start | bytes 196616 | tf_op jit(solution)/shard_map/cond/branch_2_fun/ppermute | solution.py:242
  38.8 6.8 %collective-permute-start.18 = (bf16[1,2,128,128]{3,2,1,0:T(8,128)(2,1)S(1)}, bf16[1,2,128,128]{3,2,1,0:T(8,128)(2,1)S(1)}, u32[]{:S(2)}, u32[]{:S(2)}) collective-permute-start(bf16[1,2,128,128]{3,2,1,0:T(8,128)(2,1)S(1)} %slice.90), channel_id=1, source_target_pairs={{224,352},{256,384},{288,416},{320,448},{480,96},{0,128},{32,160},... | collective-permute-start | bytes 196616 | tf_op jit(solution)/shard_map/cond/branch_2_fun/ppermute | solution.py:242
  45.6 3.0 %copy-start.12 = (f32[7,512]{1,0:T(8,128)S(1)}, f32[7,512]{1,0:T(8,128)}, u32[]{:S(2)}) copy-start(f32[7,512]{1,0:T(8,128)} %get-tuple-element.152.taps_ref) | copy-start | bytes 43012
  45.7 4.3 %collective-permute-start.19 = (bf16[1,2,128,128]{3,2,1,0:T(8,128)(2,1)S(1)}, bf16[1,2,128,128]{3,2,1,0:T(8,128)(2,1)S(1)}, u32[]{:S(2)}, u32[]{:S(2)}) collective-permute-start(bf16[1,2,128,128]{3,2,1,0:T(8,128)(2,1)S(1)} %add.20.refs_1_), channel_id=1, source_target_pairs={{0,16},{16,0},{1,17},{17,1},{2,18},{18,2},{3,19},{19,3},{4,20},{20... | collective-permute-start | bytes 196616 | tf_op jit(solution)/shard_map/cond/branch_2_fun/ppermute | solution.py:262
  54.8 5.4 %collective-permute-start.20 = (bf16[4,2,128,128]{3,2,1,0:T(8,128)(2,1)S(1)}, bf16[4,2,128,128]{3,2,1,0:T(8,128)(2,1)S(1)}, u32[]{:S(2)}, u32[]{:S(2)}) collective-permute-start(bf16[4,2,128,128]{3,2,1,0:T(8,128)(2,1)S(1)} %collective-permute-done.15.refs_0_), channel_id=1, source_target_pairs={{0,16},{16,0},{1,17},{17,1},{2,18},{18,2},{3,19},{19,3},{4,20},{20... | collective-permute-start | bytes 786440 | tf_op jit(solution)/shard_map/cond/branch_2_fun/ppermute | solution.py:265
  96.9 22.1 %all-to-all-start.19 = ((f32[32,1,128]{2,1,0:T(1,128)}), f32[32,1,128]{2,1,0:T(1,128)S(1)}, u32[]{:S(2)}, u32[]{:S(2)}) async-start(f32[32,1,128]{2,1,0:T(1,128)} %get-tuple-element.306), calls=%async_computation.19 | async-start | bytes 32768 | tf_op jit(solution)/shard_map/record_energy/all_to_all | solution.py:316
  108.8 10.3 %copy-start.29 = (s32[16]{0:T(128)S(1)}, s32[16]{0:T(128)}, u32[]{:S(2)}) copy-start(s32[16]{0:T(128)} %lengths.1) | copy-start | bytes 196

commit v4 on v1

--- a/solution.py
+++ b/solution.py
@@ -135,7 +135,7 @@
         sources = [before(refs[0], core if phase == 1 else 1 - core)]
         state, outs = refs[1:4], refs[4:]
 
-    @pl.loop(0, GROUP)
+    @pl.loop(0, GROUP, unroll=2 if phase == 2 else 1)
     def _(block):
         query_first = chip_position(cut, group, block, core, rows)
         query_pos = query_first + place

time: 119 us -> 121 us (1.017)
  waiting for transfers between devices: 30.7 us -> 32.5 us
  starting transfers between devices: 47.1 us -> 48.7 us
    all_to_all x1, starting transfers between devices: 9.78 us -> 19.8 us  [on_device(): sums = lax.all_to_all(sums, POSITIONS, 0, 0, tiled=True)]
    ppermute x3, starting transfers between devices: 10.7 us -> 3.39 us  [along(): return lax.ppermute(value, 'z', pairs)]
    ppermute x3, waiting for transfers between devices: 13.9 us -> 15.5 us  [along(): return lax.ppermute(value, 'z', pairs)]
where the time goes in v4:
time: 121 us; the launch traced here: 122 us
  starting transfers between devices  48.7 us (40%)
  waiting for transfers between devices  32.5 us (27%)
  blocking collectives  22.6 us (19%)
  Pallas kernels  15.1 us (12%)
  between operations  1.33 us (1%)
    all_to_all x1, starting transfers between devices, on_device(): sums = lax.all_to_all(sums, POSITIONS, 0, 0, tiled=True)  19.8 us
    ppermute x3, waiting for transfers between devices, along(): return lax.ppermute(value, 'z', pairs)  15.5 us
    all_to_all x1, starting transfers between devices, mixers(): lax.all_to_all(packed, 'z', 0, 0, axis_index_groups=groups, tiled=True)  14.4 us
    all_to_all x1, blocking collectives, on_device(): parts = lax.all_to_all(squares, 'mp', 0, 0, tiled=True)  13.2 us
    all_to_all x1, waiting for transfers between devices, on_device(): sums = lax.all_to_all(sums, POSITIONS, 0, 0, tiled=True)  10.1 us
    all_to_all x1, blocking collectives, mixers(): heads = lax.all_to_all(out, 'z', 0, 0, axis_index_groups=groups, tiled=True)  9.45 us
    pallas_call x3, Pallas kernels, attend(): pl.pallas_call(functools.partial(attend_kernel, long_chip, phase), out_sh...  8.02 us
    all_to_all x1, waiting for transfers between devices, mixers(): lax.all_to_all(packed, 'z', 0, 0, axis_index_groups=groups, tiled=True)  6.85 us
  transfers between devices with their start and end apart: 9, of which 4 were waited for; matrix products, arithmetic and copies ran while one was open for 0% of the time, Pallas kernels for 7%

profile of v4, /device:TPU:1, one launch (start us, length us, event | category | flops | bytes accessed | tf_op | source)
XLA Modules:
  0.0 122.2 jit_solution(1781852778779926569)
XLA Ops:
  0.6 0.0 copy-start.19
  0.6 0.0 copy-start
  0.7 0.6 copy-done.19
  1.3 1.8 %pack_heads.1 = (bf16[4,3,128,128]{3,2,1,0:T(8,128)(2,1)}, s32[2,1,128]{2,1,0:T(1,128)}, s32[1]{0:T(128)}) custom-call(s32[16]{0:T(128)S(1)} %copy-done.19, s32[16]{0:T(128)} %lengths.1, bf16[3,128,512]{2,1,0:T(8,128)(2,1)} %bitcast.13), custom_call_target="tpu_custom_call" | custom-call | tf_op jit(solution)/shard_map/pack_heads/pallas_call | solution.py:49
  3.8 0.0 copy-done
  3.8 70.8 %conditional.4 = (f32[128,512]{1,0:T(8,128)S(1)}, f32[4,128,128]{2,1,0:T(8,128)S(1)}) conditional(s32[]{:T(128)} %bitcast.1, (bf16[4,3,128,128]{3,2,1,0:T(8,128)(2,1)}, bf16[3,128,512]{2,1,0:T(8,128)(2,1)S(1)}, s32[16]{0:T(128)S(1)}, bf16[128,512]{1,0:T(8,128)(2,1)}, f32[7,512]{1,0:T(8,128)}) %tuple.148, ...), branch_computations={%region_0.0_spmd, %region_1.0_spmd, %region_2.0_spmd, %region_3.0_... | conditional | flops 4020163840 | bytes 12116380
  4.0 14.4 %all-to-all-start.8 = ((bf16[4,3,128,128]{3,2,1,0:T(8,128)(2,1)}), bf16[4,3,128,128]{3,2,1,0:T(8,128)(2,1)S(1)}, u32[]{:S(2)}, u32[]{:S(2)}) async-start(bf16[4,3,128,128]{3,2,1,0:T(8,128)(2,1)} %get-tuple-element.182), calls=%async_computation.8 | async-start | bytes 786432 | tf_op jit(solution)/shard_map/cond/branch_4_fun/all_to_all | solution.py:246
  18.4 1.9 %collective-permute-start.28 = (bf16[2,16,512]{2,1,0:T(8,128)(2,1)S(1)}, bf16[2,16,512]{2,1,0:T(8,128)(2,1)S(1)}, u32[]{:S(2)}, u32[]{:S(2)}) collective-permute-start(bf16[2,16,512]{2,1,0:T(8,128)(2,1)S(1)} %slice.69), channel_id=1, source_target_pairs={{0,16},{16,32},{32,48},{48,64},{64,80},{80,96},{96,112},{112,128},... | collective-permute-start | bytes 98312 | tf_op jit(solution)/shard_map/cond/branch_4_fun/ppermute | solution.py:245
  20.3 6.8 %all-to-all-done.8.q_ref = bf16[4,3,128,128]{3,2,1,0:T(8,128)(2,1)S(1)} async-done(((bf16[4,3,128,128]{3,2,1,0:T(8,128)(2,1)}), bf16[4,3,128,128]{3,2,1,0:T(8,128)(2,1)S(1)}, u32[]{:S(2)}, u32[]{:S(2)}) %all-to-all-start.8) | async-done | bytes 393248 | tf_op jit(solution)/shard_map/cond/branch_4_fun/all_to_all | solution.py:246
  27.2 0.0 collective-permute-done.28.rim
  27.2 0.0 copy-start.24
  27.2 4.0 %collective-permute-start.30 = (bf16[4,2,128,128]{3,2,1,0:T(8,128)(2,1)S(1)}, bf16[4,2,128,128]{3,2,1,0:T(8,128)(2,1)S(1)}, u32[]{:S(2)}, u32[]{:S(2)}) collective-permute-start(bf16[4,2,128,128]{3,2,1,0:T(8,128)(2,1)S(1)} %slice.93), channel_id=1, source_target_pairs={{0,16},{16,0},{1,17},{17,1},{2,18},{18,2},{3,19},{19,3},{4,20},{20... | collective-permute-start | bytes 786440 | tf_op jit(solution)/shard_map/cond/branch_4_fun/ppermute | solution.py:250
  31.2 1.3 %collective-permute-start.29 = (bf16[4,2,128,128]{3,2,1,0:T(8,128)(2,1)S(1)}, bf16[4,2,128,128]{3,2,1,0:T(8,128)(2,1)S(1)}, u32[]{:S(2)}, u32[]{:S(2)}) collective-permute-start(bf16[4,2,128,128]{3,2,1,0:T(8,128)(2,1)S(1)} %slice.93), channel_id=1, source_target_pairs={{160,288},{192,320},{224,352},{256,384},{416,32},{448,64},{480,96}... | collective-permute-start | bytes 786440 | tf_op jit(solution)/shard_map/cond/branch_4_fun/ppermute | solution.py:242
  32.6 0.0 copy-done.24
  32.6 0.0 copy-start.5
  32.6 0.0 collective-permute-done.30.refs_0_
  32.6 0.8 collective-permute-start.31
  33.4 1.3 %collective-permute-start.32 = (bf16[1,2,128,128]{3,2,1,0:T(8,128)(2,1)S(1)}, bf16[1,2,128,128]{3,2,1,0:T(8,128)(2,1)S(1)}, u32[]{:S(2)}, u32[]{:S(2)}) collective-permute-start(bf16[1,2,128,128]{3,2,1,0:T(8,128)(2,1)S(1)} %slice.94), channel_id=1, source_target_pairs={{32,160},{64,192},{96,224},{128,256},{288,416},{320,448},{352,480}... | collective-permute-start | bytes 196616 | tf_op jit(solution)/shard_map/cond/branch_4_fun/ppermute | solution.py:242
  34.7 0.0 collective-permute-done.31
  34.7 13.4 %collective-permute-done.32 = bf16[1,2,128,128]{3,2,1,0:T(8,128)(2,1)S(1)} collective-permute-done((bf16[1,2,128,128]{3,2,1,0:T(8,128)(2,1)S(1)}, bf16[1,2,128,128]{3,2,1,0:T(8,128)(2,1)S(1)}, u32[]{:S(2)}, u32[]{:S(2)}) %collective-permute-start.32) | collective-permute-done | bytes 65568 | tf_op jit(solution)/shard_map/cond/branch_4_fun/ppermute | solution.py:242
  48.1 0.0 copy-start.14
  48.2 2.8 %collective-permute-start.33 = (bf16[1,2,128,128]{3,2,1,0:T(8,128)(2,1)S(1)}, bf16[1,2,128,128]{3,2,1,0:T(8,128)(2,1)S(1)}, u32[]{:S(2)}, u32[]{:S(2)}) collective-permute-start(bf16[1,2,128,128]{3,2,1,0:T(8,128)(2,1)S(1)} %add.22.refs_1_), channel_id=1, source_target_pairs={{0,16},{16,0},{1,17},{17,1},{2,18},{18,2},{3,19},{19,3},{4,20},{20... | collective-permute-start | bytes 196616 | tf_op jit(solution)/shard_map/cond/branch_4_fun/ppermute | solution.py:262
  51.0 0.0 copy-done.5
  51.0 0.0 copy-done.14
  51.0 1.3 %hyena.13 = f32[128,512]{1,0:T(8,128)S(1)} custom-call(s32[16]{0:T(128)S(1)} %get-tuple-element.185.starts, bf16[128,512]{1,0:T(8,128)(2,1)S(1)} %copy-done.5, bf16[3,128,512]{2,1,0:T(8,128)(2,1)S(1)} %get-tuple-element.192.streams, bf16[2,16,512]{2,1,0:T(8,128)(2,1)} %copy-done.24, f32[7,512]{1,0:T(8,128)S(1)} %copy-done.14), custom_call_target="tpu_custom_call" | custom-call | flops 10000000 | bytes 1048576 | tf_op jit(solution)/shard_map/cond/branch_4_fun/hyena/pallas_call | solution.py:253
  52.3 0.0 collective-permute-done.33.refs_2_
  52.3 3.1 %attend0.13 = (f32[4,128,1]{2,1,0:T(8,128)S(1)}, f32[4,128,1]{2,1,0:T(8,128)S(1)}, f32[4,128,128]{2,1,0:T(8,128)S(1)}) custom-call(s32[16]{0:T(128)S(1)} %get-tuple-element.185.starts, bf16[4,3,128,128]{3,2,1,0:T(8,128)(2,1)S(1)} %all-to-all-done.8.q_ref, bf16[4,2,128,128]{3,2,1,0:T(8,128)(2,1)S(1)} %collective-permute-done.30.refs_0_, ...), custom_call_target="tpu_custom_call" | custom-call | flops 10000000 | bytes 1048576 | tf_op jit(solution)/shard_map/cond/branch_4_fun/attend0/pallas_call | solution.py:165
  55.4 2.1 %collective-permute-done.29.refs_0_ = bf16[4,2,128,128]{3,2,1,0:T(8,128)(2,1)S(1)} collective-permute-done((bf16[4,2,128,128]{3,2,1,0:T(8,128)(2,1)S(1)}, bf16[4,2,128,128]{3,2,1,0:T(8,128)(2,1)S(1)}, u32[]{:S(2)}, u32[]{:S(2)}) %collective-permute-start.29) | collective-permute-done | bytes 262176 | tf_op jit(solution)/shard_map/cond/branch_4_fun/ppermute | solution.py:242
  57.5 2.3 %collective-permute-start.34 = (bf16[4,2,128,128]{3,2,1,0:T(8,128)(2,1)S(1)}, bf16[4,2,128,128]{3,2,1,0:T(8,128)(2,1)S(1)}, u32[]{:S(2)}, u32[]{:S(2)}) collective-permute-start(bf16[4,2,128,128]{3,2,1,0:T(8,128)(2,1)S(1)} %collective-permute-done.29.refs_0_), channel_id=1, source_target_pairs={{0,16},{16,0},{1,17},{17,1},{2,18},{18,2},{3,19},{19,3},{4,20},{20... | collective-permute-start | bytes 786440 | tf_op jit(solution)/shard_map/cond/branch_4_fun/ppermute | solution.py:265
  59.9 2.6 %attend1.13 = (f32[4,128,1]{2,1,0:T(8,128)S(1)}, f32[4,128,1]{2,1,0:T(8,128)S(1)}, f32[4,128,128]{2,1,0:T(8,128)S(1)}) custom-call(s32[16]{0:T(128)S(1)} %get-tuple-element.185.starts, bf16[4,3,128,128]{3,2,1,0:T(8,128)(2,1)S(1)} %all-to-all-done.8.q_ref, bf16[4,2,128,128]{3,2,1,0:T(8,128)(2,1)S(1)} %collective-permute-done.29.refs_0_, ...), custom_call_target="tpu_custom_call" | custom-call | flops 2000000000 | bytes 1048576 | tf_op jit(solution)/shard_map/cond/branch_4_fun/attend1/pallas_call | solution.py:165
  62.5 0.0 collective-permute-done.34.refs_0_
  62.5 2.4 %attend2.13 = f32[4,128,128]{2,1,0:T(8,128)S(1)} custom-call(s32[16]{0:T(128)S(1)} %get-tuple-element.185.starts, bf16[4,3,128,128]{3,2,1,0:T(8,128)(2,1)S(1)} %all-to-all-done.8.q_ref, bf16[4,2,128,128]{3,2,1,0:T(8,128)(2,1)S(1)} %collective-permute-done.34.refs_0_, f32[4,128,1]{2,1,0:T(8,128)S(1)} %get-tuple-element.200.refs_1_, ...), custom_call_target="tpu_custom_call" | custom-call | flops 2000000000 | bytes 1048576 | tf_op jit(solution)/shard_map/cond/branch_4_fun/attend2/pallas_call | solution.py:165
  64.9 9.4 %all_to_all.86 = f16[4,128,128]{2,1,0:T(8,128)(2,1)S(1)} all-to-all(f16[4,128,128]{2,1,0:T(8,128)(2,1)S(1)} %convert_element_type.66), channel_id=1, replica_groups={{32,64,96,128},{160,192,224,256},{288,320,352,384},{416,448,480,0},{33,..., dimensions={0} | all-to-all | bytes 262144 | tf_op jit(solution)/shard_map/cond/branch_4_fun/all_to_all | solution.py:269
  74.6 0.7 stream.1
  75.4 13.2 %all_to_all.91.parts = f32[16,1,128]{2,1,0:T(1,128)} all-to-all(f32[16,1,128]{2,1,0:T(1,128)} %get-tuple-element.304), channel_id=1, replica_groups=mesh['z'=16,'core'=2,'mp'=16] {'mp'}, dimensions={0} | all-to-all | bytes 16384 | tf_op jit(solution)/shard_map/mean_square/all_to_all | solution.py:306
  88.6 1.4 %records.1 = (f32[128,128]{1,0:T(8,128)}, f32[32,1,128]{2,1,0:T(1,128)}) custom-call(s32[2,1,128]{2,1,0:T(1,128)} %get-tuple-element.303.lines, f32[16,1,128]{2,1,0:T(1,128)} %all_to_all.91.parts), custom_call_target="tpu_custom_call" | custom-call | tf_op jit(solution)/shard_map/record_energy/records/pallas_call | solution.py:308
  90.0 19.8 %all-to-all-start.19 = ((f32[32,1,128]{2,1,0:T(1,128)}), f32[32,1,128]{2,1,0:T(1,128)S(1)}, u32[]{:S(2)}, u32[]{:S(2)}) async-start(f32[32,1,128]{2,1,0:T(1,128)} %get-tuple-element.306), calls=%async_computation.19 | async-start | bytes 32768 | tf_op jit(solution)/shard_map/record_energy/all_to_all | solution.py:316
  109.8 1.7 %scale.1 = f32[128,512]{1,0:T(8,128)} custom-call(f32[128,512]{1,0:T(8,128)} %get-tuple-element.302.stream, f32[128,128]{1,0:T(8,128)} %get-tuple-element.305.mean, f32[1,512]{1,0:T(1,128)} %bitcast.14), custom_call_target="tpu_custom_call" | custom-call | flops 1000000000 | bytes 1048576 | tf_op jit(solution)/shard_map/scale/pallas_call | solution.py:318
  111.6 0.0 copy-start.29
  111.6 10.1 %all-to-all-done.19 = f32[32,1,128]{2,1,0:T(1,128)S(1)} async-done(((f32[32,1,128]{2,1,0:T(1,128)}), f32[32,1,128]{2,1,0:T(1,128)S(1)}, u32[]{:S(2)}, u32[]{:S(2)}) %all-to-all-start.19) | async-done | bytes 16416 | tf_op jit(solution)/shard_map/record_energy/all_to_all | solution.py:316
  121.7 0.1 reduce_sum.9
  121.7 0.0 copy-done.29
  121.7 0.5 convert_divide_fusion
  (6 shorter events, 0.1 us)
Async XLA Ops:
  0.6 0.7 copy-start.19
  0.6 3.1 %copy-start = (bf16[128,3,512]{2,0,1:T(8,128)(2,1)S(1)}, bf16[128,3,512]{2,0,1:T(8,128)(2,1)}, u32[]{:S(2)}) copy-start(bf16[128,3,512]{2,0,1:T(8,128)(2,1)} %param.18) | copy-start | bytes 1179652
  4.0 23.1 %all-to-all-start.8 = ((bf16[4,3,128,128]{3,2,1,0:T(8,128)(2,1)}), bf16[4,3,128,128]{3,2,1,0:T(8,128)(2,1)S(1)}, u32[]{:S(2)}, u32[]{:S(2)}) async-start(bf16[4,3,128,128]{3,2,1,0:T(8,128)(2,1)} %get-tuple-element.182), calls=%async_computation.8 | async-start | bytes 786432 | tf_op jit(solution)/shard_map/cond/branch_4_fun/all_to_all | solution.py:246
  18.4 8.8 %collective-permute-start.28 = (bf16[2,16,512]{2,1,0:T(8,128)(2,1)S(1)}, bf16[2,16,512]{2,1,0:T(8,128)(2,1)S(1)}, u32[]{:S(2)}, u32[]{:S(2)}) collective-permute-start(bf16[2,16,512]{2,1,0:T(8,128)(2,1)S(1)} %slice.69), channel_id=1, source_target_pairs={{0,16},{16,32},{32,48},{48,64},{64,80},{80,96},{96,112},{112,128},... | collective-permute-start | bytes 98312 | tf_op jit(solution)/shard_map/cond/branch_4_fun/ppermute | solution.py:245
  27.2 5.4 %copy-start.24 = (bf16[2,16,512]{2,1,0:T(8,128)(2,1)}, bf16[2,16,512]{2,1,0:T(8,128)(2,1)S(1)}, u32[]{:S(2)}) copy-start(bf16[2,16,512]{2,1,0:T(8,128)(2,1)S(1)} %collective-permute-done.28.rim) | copy-start | bytes 98308
  27.2 5.4 %collective-permute-start.30 = (bf16[4,2,128,128]{3,2,1,0:T(8,128)(2,1)S(1)}, bf16[4,2,128,128]{3,2,1,0:T(8,128)(2,1)S(1)}, u32[]{:S(2)}, u32[]{:S(2)}) collective-permute-start(bf16[4,2,128,128]{3,2,1,0:T(8,128)(2,1)S(1)} %slice.93), channel_id=1, source_target_pairs={{0,16},{16,0},{1,17},{17,1},{2,18},{18,2},{3,19},{19,3},{4,20},{20... | collective-permute-start | bytes 786440 | tf_op jit(solution)/shard_map/cond/branch_4_fun/ppermute | solution.py:250
  31.2 26.3 %collective-permute-start.29 = (bf16[4,2,128,128]{3,2,1,0:T(8,128)(2,1)S(1)}, bf16[4,2,128,128]{3,2,1,0:T(8,128)(2,1)S(1)}, u32[]{:S(2)}, u32[]{:S(2)}) collective-permute-start(bf16[4,2,128,128]{3,2,1,0:T(8,128)(2,1)S(1)} %slice.93), channel_id=1, source_target_pairs={{160,288},{192,320},{224,352},{256,384},{416,32},{448,64},{480,96}... | collective-permute-start | bytes 786440 | tf_op jit(solution)/shard_map/cond/branch_4_fun/ppermute | solution.py:242
  32.6 18.4 %copy-start.5 = (bf16[128,512]{1,0:T(8,128)(2,1)S(1)}, bf16[128,512]{1,0:T(8,128)(2,1)}, u32[]{:S(2)}) copy-start(bf16[128,512]{1,0:T(8,128)(2,1)} %get-tuple-element.191.residual) | copy-start | bytes 393220
  32.6 2.1 %collective-permute-start.31 = (bf16[1,2,128,128]{3,2,1,0:T(8,128)(2,1)S(1)}, bf16[1,2,128,128]{3,2,1,0:T(8,128)(2,1)S(1)}, u32[]{:S(2)}, u32[]{:S(2)}) collective-permute-start(bf16[1,2,128,128]{3,2,1,0:T(8,128)(2,1)S(1)} %slice.94), channel_id=1, source_target_pairs={{32,288},{64,320},{96,352},{128,384},{288,32},{320,64},{352,96},{3... | collective-permute-start | bytes 196616 | tf_op jit(solution)/shard_map/cond/branch_4_fun/ppermute | solution.py:242
  33.4 14.7 %collective-permute-start.32 = (bf16[1,2,128,128]{3,2,1,0:T(8,128)(2,1)S(1)}, bf16[1,2,128,128]{3,2,1,0:T(8,128)(2,1)S(1)}, u32[]{:S(2)}, u32[]{:S(2)}) collective-permute-start(bf16[1,2,128,128]{3,2,1,0:T(8,128)(2,1)S(1)} %slice.94), channel_id=1, source_target_pairs={{32,160},{64,192},{96,224},{128,256},{288,416},{320,448},{352,480}... | collective-permute-start | bytes 196616 | tf_op jit(solution)/shard_map/cond/branch_4_fun/ppermute | solution.py:242
  48.1 2.9 %copy-start.14 = (f32[7,512]{1,0:T(8,128)S(1)}, f32[7,512]{1,0:T(8,128)}, u32[]{:S(2)}) copy-start(f32[7,512]{1,0:T(8,128)} %get-tuple-element.194.taps_ref) | copy-start | bytes 43012
  48.2 4.2 %collective-permute-start.33 = (bf16[1,2,128,128]{3,2,1,0:T(8,128)(2,1)S(1)}, bf16[1,2,128,128]{3,2,1,0:T(8,128)(2,1)S(1)}, u32[]{:S(2)}, u32[]{:S(2)}) collective-permute-start(bf16[1,2,128,128]{3,2,1,0:T(8,128)(2,1)S(1)} %add.22.refs_1_), channel_id=1, source_target_pairs={{0,16},{16,0},{1,17},{17,1},{2,18},{18,2},{3,19},{19,3},{4,20},{20... | collective-permute-start | bytes 196616 | tf_op jit(solution)/shard_map/cond/branch_4_fun/ppermute | solution.py:262
  57.5 4.9 %collective-permute-start.34 = (bf16[4,2,128,128]{3,2,1,0:T(8,128)(2,1)S(1)}, bf16[4,2,128,128]{3,2,1,0:T(8,128)(2,1)S(1)}, u32[]{:S(2)}, u32[]{:S(2)}) collective-permute-start(bf16[4,2,128,128]{3,2,1,0:T(8,128)(2,1)S(1)} %collective-permute-done.29.refs_0_), channel_id=1, source_target_pairs={{0,16},{16,0},{1,17},{17,1},{2,18},{18,2},{3,19},{19,3},{4,20},{20... | collective-permute-start | bytes 786440 | tf_op jit(solution)/shard_map/cond/branch_4_fun/ppermute | solution.py:265
  90.0 31.7 %all-to-all-start.19 = ((f32[32,1,128]{2,1,0:T(1,128)}), f32[32,1,128]{2,1,0:T(1,128)S(1)}, u32[]{:S(2)}, u32[]{:S(2)}) async-start(f32[32,1,128]{2,1,0:T(1,128)} %get-tuple-element.306), calls=%async_computation.19 | async-start | bytes 32768 | tf_op jit(solution)/shard_map/record_energy/all_to_all | solution.py:316
  111.6 10.1 %copy-start.29 = (s32[16]{0:T(128)S(1)}, s32[16]{0:T(128)}, u32[]{:S(2)}) copy-start(s32[16]{0:T(128)} %lengths.1) | copy-start | bytes 196
